TPU v7x, 256 devices: a whole 4x4x8 slice. The times are simulated.
256 devices in a mesh: dp: 32 (over z_lo, x, core), space: 8 (over y, z_hi).
Axes of the slice: x: 4, y: 4, z: 8 (z_hi: 2, z_lo: 4; z = z_hi * 4 + z_lo), core: 2. Of those that a mesh axis runs over, the one named last changes fastest.
Arguments:
- volumes: bfloat16 [32, 32, 32, 16, 128], P('dp', None, 'space'), may hold values from -6 to 6
- w_first: bfloat16 [27, 32, 64], replicated, may hold values from -0.21875 to 0.21875
- w_second: bfloat16 [27, 64, 64], replicated, may hold values from -0.15625 to 0.15625
- grad_out: bfloat16 [32, 64, 16, 8, 64], P('dp', 'space'), may hold values from -6 to 6
Outputs:
- features: bfloat16 [32, 64, 16, 8, 64], P('dp', 'space')
- grad_first: float32 [27, 32, 64], replicated
- grad_second: float32 [27, 64, 64], replicated
All inputs are finite; a program needn't handle non-finite values.
Results may differ from a plain program's by a relative error of at most 0.0049.
Values may be sent and summed in bfloat16 or wider, within the bound.
No kernel may reach another device: no remote copies, remote signals or barrier semaphores. Data moves between devices by JAX's collectives and lax.ppermute only.
A program may use at most 64 MiB of HBM per device.

v0:
```python
import jax
import jax.numpy as jnp
from jax import lax
from jax.sharding import PartitionSpec as P

SLOPE = 0.3
FWD = ("NCDHW", "DHWIO", "NCDHW")
WGRAD = ("CNDHW", "IODHW", "DHWNC")


def passed_along(value, axis, steps):
    count = lax.axis_size(axis)
    initial, last = (max(0, -steps), min(count, count - steps))
    return lax.ppermute(value, axis, [(source, source + steps) for source in range(initial, last)])


def convolve(lhs, rhs, stride, pads, specs, dilation):
    return lax.conv_general_dilated(
        lhs,
        rhs,
        (stride, stride, stride),
        pads,
        rhs_dilation=(dilation, dilation, dilation),
        dimension_numbers=specs,
        preferred_element_type=jnp.float32,
    )


def shards(volumes, w_first, w_second, grad_out):
    count_in = w_first.shape[1]
    count_out = w_first.shape[2]
    depth = volumes.shape[2]
    kernel_one = w_first.reshape(3, 3, 3, count_in, count_out)
    kernel_two = w_second.reshape(3, 3, 3, count_out, count_out)
    flipped = jnp.transpose(kernel_two[::-1, ::-1, ::-1], (0, 1, 2, 4, 3))
    lower = passed_along(volumes[:, :, depth - 1 :], "space", 1)
    extended = jnp.concatenate([lower, volumes], axis=2)
    pre = convolve(extended, kernel_one, 2, [(0, 0), (1, 1), (1, 1)], FWD, 1)
    act = jnp.where(pre > 0, pre, SLOPE * pre).astype(jnp.bfloat16)
    groups = lax.axis_size("space")
    share = count_out // groups
    first_channel = lax.axis_index("space") * share
    full_act = lax.all_gather(act, "space", axis=2, tiled=True)
    own_cols = lax.dynamic_slice_in_dim(kernel_two, first_channel, share, 4)
    features = convolve(full_act, own_cols, 1, [(1, 1)] * 3, FWD, 1).astype(jnp.bfloat16)
    full_grad = lax.all_gather(grad_out, "space", axis=1, tiled=True)
    own_flip = lax.dynamic_slice_in_dim(flipped, first_channel, share, 4)
    grad_own = convolve(full_grad, own_flip, 1, [(1, 1)] * 3, FWD, 1).astype(jnp.bfloat16)
    grad_act = lax.all_to_all(grad_own, "space", split_axis=2, concat_axis=1, tiled=True)
    own_act = lax.dynamic_slice_in_dim(full_act, first_channel, share, 1)
    grad_rows = convolve(own_act, full_grad, 1, [(1, 1)] * 3, WGRAD, 1)
    whole_two = lax.dynamic_update_slice_in_dim(
        jnp.zeros((3, 3, 3, count_out, count_out), jnp.float32), grad_rows, first_channel, 3
    )
    grad_pre = (grad_act.astype(jnp.float32) * jnp.where(pre > 0, 1.0, SLOPE)).astype(jnp.bfloat16)
    whole_one = convolve(extended, grad_pre, 1, [(0, 0), (1, 0), (1, 0)], WGRAD, 2)
    total_one, total_two = lax.psum(
        (whole_one.reshape(27, count_in, count_out), whole_two.reshape(27, count_out, count_out)),
        ("dp", "space"),
    )
    return (features, total_one, total_two)


def solution(mesh):
    placed = (P("dp", None, "space", None, None), P(), P(), P("dp", "space", None, None, None))
    return jax.shard_map(
        shards,
        mesh=mesh,
        in_specs=placed,
        out_specs=(P("dp", "space", None, None, None), P(), P()),
        check_vma=False,
    )
```

profile of v0, /device:TPU:1, one launch (start us, length us, event | category | flops | bytes accessed | tf_op | source)
XLA Modules:
  0.0 545.7 jit_solution(102058875730480440)
XLA Ops:
  8.0 0.9 slice.3
  8.9 9.7 %collective-permute-start = (bf16[1,32,1,16,128]{4,3,2,1,0:T(8,128)(2,1)S(1)}, bf16[1,32,1,16,128]{4,3,2,1,0:T(8,128)(2,1)S(1)}, u32[]{:S(2)}, u32[]{:S(2)}) collective-permute-start(bf16[1,32,1,16,128]{4,3,2,1,0:T(8,128)(2,1)S(1)} %slice.3), channel_id=1, source_target_pairs={{0,1},{1,2},{2,3},{3,4},{4,5},{5,6},{6,7},{8,9},{9,10},{10,11},{11... | collective-permute-start | bytes 393224 | tf_op jit(solution)/shard_map/ppermute | solution.py:14
  18.5 2.2 collective-permute-done
  20.8 1.1 constant_dynamic-update-slice_fusion
  21.9 3.4 copy.92
  25.8 1.1 copy.66
  27.1 2.0 compare_select_fusion
  29.2 0.9 copy.68
  30.5 5.7 %copy.85 = bf16[1,32,5,16,128]{1,0,4,3,2:T(2,128)(2,1)} copy(bf16[1,32,5,16,128]{4,3,2,1,0:T(8,128)(2,1)S(1)} %constant_dynamic-update-slice_fusion) | data formatting | bytes 1310720 | tf_op jit(solution)/shard_map/concatenate | solution.py:37
  36.3 1.1 copy.90
  37.5 52.0 %all-gather.5.cloned.1.call-done = bf16[1,64,16,8,64]{4,3,2,0,1:T(8,128)(2,1)} async-done(((bf16[1,8,16,8,64]{4,3,2,0,1:T(8,128)(2,1)}), bf16[1,64,16,8,64]{4,3,2,0,1:T(8,128)(2,1)}) %all-gather.5.cloned.1.call-update) | async-done | bytes 1048592 | tf_op jit(solution)/shard_map/all_gather | solution.py:46
  89.4 4.1 copy.94
  94.8 10.8 %fusion.13 = bf16[16,8,8,9,8]{4,2,3,1,0:T(8,128)(2,1)} fusion(bf16[64,16,8,1,7,2]{0,4,5,2,1,3:T(8,128)(2,1)S(1)} %slice.15, bf16[64,16,8,1,8,9]{0,4,5,2,1,3:T(8,128)(2,1)S(1)} %copy.78, bf16[3,3,3,64,64]{3,4,2,1,0:T(8,128)(2,1)S(1)} %rev.3, s32[]{:T(128)S(6)} %select_n.15), kind=kOutput, calls=%fused_computation.13 | convolution fusion | flops 228163584 | bytes 1777668 | tf_op jit(solution)/shard_map/conv_general_dilated | solution.py:18
  105.6 4.0 copy.79
  109.5 7.6 %copy.88 = bf16[1,64,16,8,64]{1,0,4,3,2:T(2,128)(2,1)} copy(bf16[1,64,16,8,64]{4,3,2,0,1:T(8,128)(2,1)S(1)} %copy-done.2) | data formatting | bytes 2097152 | tf_op jit(solution)/shard_map/all_gather | solution.py:46
  117.2 47.3 %all-gather.3.cloned.1.call-done = bf16[1,64,16,8,64]{4,3,1,0,2:T(8,128)(2,1)} async-done(((bf16[1,64,2,8,64]{4,3,1,0,2:T(8,128)(2,1)}), bf16[1,64,16,8,64]{4,3,1,0,2:T(8,128)(2,1)}) %all-gather.3.cloned.1.call-update) | async-done | bytes 1048592 | tf_op jit(solution)/shard_map/all_gather | solution.py:43
  164.4 3.5 copy.96
  167.9 4.1 copy.93
  173.3 18.8 %fusion.9 = bf16[16,8,8,9,8]{4,2,3,1,0:T(8,128)(2,1)} fusion(bf16[64,16,8,1,7,2]{0,4,5,2,1,3:T(8,128)(2,1)S(1)} %slice.13, bf16[64,16,8,1,8,9]{0,4,5,2,1,3:T(8,128)(2,1)S(1)} %copy.72, bf16[3,3,3,64,64]{3,4,2,1,0:T(8,128)(2,1)} %bitcast.65, s32[]{:T(128)S(6)} %select_n.15), kind=kOutput, calls=%fused_computation.10 | convolution fusion | flops 228163584 | bytes 1611780 | tf_op jit(solution)/shard_map/conv_general_dilated | solution.py:18
  192.1 3.8 copy.74
  196.0 1.6 select_convert_fusion
  197.6 1.0 copy.80
  199.5 3.4 all-to-all-start
  202.9 1.0 constant_dynamic-slice_fusion
  203.9 7.5 %copy.91 = bf16[1,8,16,8,64]{1,0,4,3,2:T(2,128)(2,1)} copy(bf16[1,8,16,8,64]{4,3,1,0,2:T(8,128)(2,1)S(1)} %constant_dynamic-slice_fusion) | data formatting | bytes 262144
  211.4 46.5 %convolution_dynamic-update-slice_fusion = f32[3,3,3,64,64]{4,3,2,1,0:T(8,128)S(1)} fusion(f32[3,3,3,64,64]{4,3,2,1,0:T(8,128)S(1)} %broadcast_in_dim.10, s32[]{:T(128)S(6)} %select_n.15, bf16[1,8,16,8,64]{1,0,4,3,2:T(2,128)(2,1)} %copy.91, bf16[1,64,16,8,64]{1,0,4,3,2:T(2,128)(2,1)} %copy.88), kind=kOutput, calls=%fused_computation.27 | convolution fusion | flops 196894720 | bytes 1290244 | tf_op jit(solution)/shard_map/conv_general_dilated | solution.py:18
  258.3 1.0 copy-done.5
  260.1 14.1 %fusion.42 = f32[3,3,3,32,64]{4,3,2,1,0:T(8,128)} fusion(bf16[1,32,5,16,128]{1,0,4,3,2:T(2,128)(2,1)} %copy.85, bf16[1,64,2,8,64]{1,0,4,3,2:T(2,128)(2,1)S(1)} %copy.86), kind=kOutput, calls=%fused_computation.53 | convolution fusion | flops 107962368 | bytes 1007616 | tf_op jit(solution)/shard_map/conv_general_dilated | solution.py:18
  274.3 1.5 copy.89
  275.8 259.0 %all-reduce.3.cloned.1.call-done = (f32[27,32,64]{2,1,0:T(8,128)}, f32[27,64,64]{2,1,0:T(8,128)}) async-done(((f32[27,32,64]{2,1,0:T(8,128)}, f32[27,64,64]{2,1,0:T(8,128)}), (f32[27,32,64]{2,1,0:T(8,128)}, f32[27,64,64]{2,1,0:T(8,128)})) %all-reduce.3.cloned.1.call-update) | async-done | bytes 663568 | tf_op jit(solution)/shard_map/psum | solution.py:57
  534.7 1.8 copy.101
  536.5 2.2 copy.102
  (51 shorter events, 6.7 us)
Async XLA Ops:
  7.2 19.9 %copy-start = (bf16[27,32,64]{2,1,0:T(8,128)(2,1)S(1)}, bf16[27,32,64]{2,1,0:T(8,128)(2,1)}, u32[]{:S(2)}) copy-start(bf16[27,32,64]{2,1,0:T(8,128)(2,1)} %param.5) | copy-start | bytes 331780
  7.2 82.2 %all-gather.5.cloned.1.call-start = ((), (), s32[]{:S(2)}) async-start(), calls=%async_computation.2 | async-start | bytes 2359296 | tf_op jit(solution)/shard_map/all_gather | solution.py:46
  7.9 156.5 %all-gather.3.cloned.1.call-start = ((), (), s32[]{:S(2)}) async-start(), calls=%async_computation.1 | async-start | bytes 2359296 | tf_op jit(solution)/shard_map/all_gather | solution.py:43
  8.9 11.9 %collective-permute-start = (bf16[1,32,1,16,128]{4,3,2,1,0:T(8,128)(2,1)S(1)}, bf16[1,32,1,16,128]{4,3,2,1,0:T(8,128)(2,1)S(1)}, u32[]{:S(2)}, u32[]{:S(2)}) collective-permute-start(bf16[1,32,1,16,128]{4,3,2,1,0:T(8,128)(2,1)S(1)} %slice.3), channel_id=1, source_target_pairs={{0,1},{1,2},{2,3},{3,4},{4,5},{5,6},{6,7},{8,9},{9,10},{10,11},{11... | collective-permute-start | bytes 393224 | tf_op jit(solution)/shard_map/ppermute | solution.py:14
  25.8 1.3 copy-start.9
  27.1 3.1 copy-start.7
  30.4 5.8 %copy-start.6 = (bf16[27,64,64]{1,2,0:T(8,128)(2,1)}, bf16[27,64,64]{1,2,0:T(8,128)(2,1)S(1)}, u32[]{:S(2)}) copy-start(bf16[27,64,64]{1,2,0:T(8,128)(2,1)S(1)} %copy.73) | copy-start | bytes 663556
  105.6 4.0 copy-start.2
  192.1 3.8 copy-start.8
  199.5 58.5 %all-to-all-start = ((bf16[8,2,4096]{2,1,0:T(2,128)(2,1)}), bf16[8,2,4096]{2,1,0:T(2,128)(2,1)S(1)}, u32[]{:S(2)}, u32[]{:S(2)}) async-start(bf16[8,2,4096]{2,1,0:T(2,128)(2,1)} %reshape.76), calls=%async_computation | async-start | bytes 262144 | tf_op jit(solution)/shard_map/all_to_all | solution.py:49
  202.8 331.9 %all-reduce.3.cloned.1.call-start = ((), (), s32[]{:S(2)}) async-start(), calls=%async_computation.3 | async-start | bytes 2654208 | tf_op jit(solution)/shard_map/psum | solution.py:57
  257.9 16.2 %copy-start.4 = (f32[3,3,3,64,64]{4,3,2,1,0:T(8,128)}, f32[3,3,3,64,64]{4,3,2,1,0:T(8,128)S(1)}, u32[]{:S(2)}) copy-start(f32[3,3,3,64,64]{4,3,2,1,0:T(8,128)S(1)} %convolution_dynamic-update-slice_fusion) | copy-start | bytes 1327108
  257.9 1.4 copy-start.5
  260.1 14.1 %copy-start.3 = (bf16[16,8,8,9,8]{0,4,3,2,1:T(8,128)(2,1)S(1)}, bf16[16,8,8,9,8]{0,4,3,2,1:T(8,128)(2,1)}, u32[]{:S(2)}) copy-start(bf16[16,8,8,9,8]{0,4,3,2,1:T(8,128)(2,1)} %get-tuple-element.17) | copy-start | bytes 442372
  274.2 264.5 %copy-start.1 = (bf16[27,32,64]{2,1,0:T(8,128)(2,1)S(1)}, bf16[27,32,64]{2,1,0:T(8,128)(2,1)}, u32[]{:S(2)}) copy-start(bf16[27,32,64]{2,1,0:T(8,128)(2,1)} %param.5) | copy-start | bytes 331780
Sparse Core Ops, SparseCore 0:
  10.6 78.7 all-gather.4
  92.6 71.7 all-gather.2
  274.3 260.3 all-reduce.2
where the time goes:
time: 552 us; the launch traced here: 546 us
  waiting for transfers between devices  361 us (65%)
  matrix products  92.1 us (17%)
  local copies, waits for them, and re-layouts  63.1 us (11%)
  between operations  14.6 us (3%)
  starting transfers between devices  13.1 us (2%)
    psum x1, waiting for transfers between devices, shards(): lax.psum((whole_one.reshape(27, count_in, count_out), whole_two.reshape(2...  259 us
    conv_general_dilated x5, matrix products, convolve(): lax.conv_general_dilated(lhs, rhs, (stride, stride, stride), pads, rhs_di...  92.1 us
    all_gather x1, waiting for transfers between devices, shards(): full_grad = lax.all_gather(grad_out, 'space', axis=1, tiled=True)  52 us
    all_gather x1, waiting for transfers between devices, shards(): full_act = lax.all_gather(act, 'space', axis=2, tiled=True)  47.3 us
    unnamed x32, local copies, waits for them, and re-layouts  28.1 us
  transfers between devices with their start and end apart: 5, of which 4 were waited for; matrix products, arithmetic and copies ran while one was open for 19% of the time, Pallas kernels for 0%

commit v1 on v0

v1 whole, which is shorter than its diff:
```python
import jax
import jax.numpy as jnp
import numpy as np
from jax import lax
from jax.experimental import pallas as pl
from jax.experimental.pallas import tpu as pltpu
from jax.sharding import Mesh, PartitionSpec as P

SLOPE = 0.3
BF = jnp.bfloat16
F = jnp.float32
C0, C1 = 32, 64
CELLS = 512
SLAB = 2 * CELLS
ROWS = 1536
HALF = ROWS // 2
LIMIT = 48 * 1024 * 1024


def call(kernel, outs, scratch=(), flops=0, moved=0):
    return pl.pallas_call(
        kernel,
        out_shape=outs,
        scratch_shapes=list(scratch),
        compiler_params=pltpu.CompilerParams(vmem_limit_bytes=LIMIT),
        cost_estimate=pl.CostEstimate(flops=flops, bytes_accessed=moved, transcendentals=0),
    )


def lanes(shape):
    return lax.broadcasted_iota(jnp.int32, shape, 1)


def low_half(shape):
    return lanes(shape) < 64


def cell_index(shape):
    lane = lanes(shape)
    return (lane // 64) % 8, lane % 64


def shifted(value, row, rows, col, cols):
    width = value.shape[1]
    moved = pltpu.roll(value, (-(64 * rows + cols)) % width, 1)
    inside = (row + rows >= 0) & (row + rows < 8) & (col + cols >= 0) & (col + cols < 64)
    return jnp.where(inside, moved, 0.0)


def nine_shifts(act, store):
    row, col = cell_index(act.shape)
    for c in range(3):
        side = act if c == 1 else shifted(act, row, 0, col, c - 1)
        for b in range(3):
            store(3 * b + c, side if b == 1 else shifted(side, row, b - 1, col, 0))


def pack_cotangent(x_ref, o_ref, flat):
    flat[:, 0:64] = x_ref[0].astype(F).reshape(1024, 64)
    low = low_half((8, 128))
    zero = jnp.zeros((8, CELLS), BF)
    o_ref[0, :, 0:CELLS] = zero
    o_ref[7, :, 3 * CELLS :] = zero
    for plane in range(16):
        tiles = []
        for pair in range(4):
            first = flat[pl.ds(plane * 8 + 2 * pair, 8, stride=128), :]
            second = flat[pl.ds(plane * 8 + 2 * pair + 1, 8, stride=128), :]
            tiles.append(jnp.where(low, first, pltpu.roll(second, 64, 1)))
        value = jnp.concatenate(tiles, axis=1).astype(BF)
        for slab in range(8):
            slot = plane - 2 * slab + 1
            if 0 <= slot < 4:
                o_ref[slab, :, slot * CELLS : (slot + 1) * CELLS] = value


def first_block(v_ref, h_ref, w_ref, u_ref, x_ref, act_ref, pos_ref, own, halo):
    source = lax.broadcasted_iota(jnp.int32, (128, 128), 0)
    target = lanes((128, 128))
    pick = jnp.where(target < 64, 2 * target, 2 * target - 127)
    split = (source == pick).astype(F).astype(BF)
    own[...] = jnp.dot(v_ref[0].reshape(2048, 128), split, preferred_element_type=F)
    halo[...] = jnp.dot(h_ref[0].reshape(512, 128), split, preferred_element_type=F)
    low = low_half((C0, 128))
    row, col = cell_index((C0, CELLS))

    def line(plane, at):
        if plane == 0:
            return halo[pl.ds(at, C0, stride=16), :]
        return own[pl.ds((plane - 1) * 16 + at, C0, stride=64), :]

    for plane in range(5):
        phase = {}
        for odd in range(2):
            even_cols, odd_cols = [], []
            for pair in range(4):
                first, second = line(plane, 4 * pair + odd), line(plane, 4 * pair + 2 + odd)
                even_cols.append(jnp.where(low, first, pltpu.roll(second, 64, 1)))
                odd_cols.append(jnp.where(low, pltpu.roll(first, 64, 1), second))
            phase[odd, 0] = jnp.concatenate(even_cols, axis=1)
            phase[odd, 1] = jnp.concatenate(odd_cols, axis=1)
        left = [shifted(phase[odd, 1], row, 0, col, -1) for odd in range(2)]
        taps = {
            (1, 1): phase[0, 0],
            (1, 2): phase[0, 1],
            (1, 0): left[0],
            (2, 1): phase[1, 0],
            (2, 2): phase[1, 1],
            (2, 0): left[1],
            (0, 1): shifted(phase[1, 0], row, -1, col, 0),
            (0, 2): shifted(phase[1, 1], row, -1, col, 0),
            (0, 0): shifted(left[1], row, -1, col, 0),
        }
        for (b, c), value in taps.items():
            value = value.astype(BF)
            for depth in range(2):
                a = plane - 2 * depth
                if 0 <= a < 3:
                    at = (9 * a + 3 * b + c) * C0
                    u_ref[at : at + C0, depth * CELLS : (depth + 1) * CELLS] = value
    pre = lax.dot_general(w_ref[...], u_ref[...], (((0,), (0,)), ((), ())), preferred_element_type=F)
    positive = pre > 0
    act = jnp.where(positive, pre, SLOPE * pre).astype(BF)
    act_ref[...] = act
    pos_ref[...] = positive.astype(F).astype(BF)

    def store(offset, value):
        x_ref[offset * C1 : (offset + 1) * C1, :] = value.astype(BF)

    nine_shifts(act.astype(F), store)


def gradients(core_ref, u_ref, x_ref, pos_ref, g_ref, w_ref, mine_ref, other_ref, depths, both):
    for a in range(3):
        depths[a * C1 : (a + 1) * C1, :] = g_ref[:, (2 - a) * CELLS : (2 - a) * CELLS + SLAB]
    shape = (C1, SLAB)
    row, col = cell_index(shape)
    kernel = jnp.concatenate([w_ref[a * 576 : (a + 1) * 576, :] for a in range(3)], axis=1)
    spread = jnp.dot(kernel, depths[...], preferred_element_type=F)
    total = None
    for c in range(3):
        side = None
        for b in range(3):
            at = (3 * b + c) * C1
            part = spread[at : at + C1, :]
            part = part if b == 1 else shifted(part, row, 1 - b, col, 0)
            side = part if side is None else side + part
        side = side if c == 1 else shifted(side, row, 0, col, 1 - c)
        total = side if total is None else total + side
    grad_act = total.astype(BF).astype(F)
    grad_pre = (grad_act * jnp.where(pos_ref[...].astype(F) > 0, 1.0, SLOPE)).astype(BF)
    across = (((1,), (1,)), ((), ()))
    second = lax.dot_general(x_ref[...], depths[...], across, preferred_element_type=F)
    first = lax.dot_general(u_ref[...], grad_pre, across, preferred_element_type=F)
    both[0:576, :] = second[:, 0:128]
    both[576:864, :] = jnp.concatenate([second[0:288, 128:192], second[288:576, 128:192]], axis=1)
    both[864:1296, :] = jnp.concatenate([first[0:432, :], first[432:864, :]], axis=1)
    both[1296:ROWS, :] = jnp.zeros((ROWS - 1296, 128), F)
    core = core_ref[0]
    mine_ref[...] = both[pl.ds(pl.multiple_of(core * HALF, HALF), HALF), :]
    other_ref[...] = both[pl.ds(pl.multiple_of((1 - core) * HALF, HALF), HALF), :]


def second_block(x_ref, below_ref, above_ref, w_ref, o_ref, planes):
    planes[:, CELLS : 3 * CELLS] = x_ref[...]

    def store(offset, value):
        at = offset * C1
        value = value.astype(BF)
        planes[at : at + C1, 0:CELLS] = value[:, 0:CELLS]
        planes[at : at + C1, 3 * CELLS :] = value[:, CELLS:]

    nine_shifts(jnp.concatenate([below_ref[...], above_ref[...]], axis=1).astype(F), store)
    total = None
    for a in range(3):
        part = lax.dot_general(
            w_ref[a * 576 : (a + 1) * 576, :],
            planes[:, a * CELLS : a * CELLS + SLAB],
            (((0,), (0,)), ((), ())),
            preferred_element_type=F,
        )
        total = part if total is None else total + part
    o_ref[...] = total.astype(BF)


def unpack_features(x_ref, o_ref, flat):
    for slab in range(8):
        value = x_ref[slab].astype(F)
        for depth in range(2):
            for pair in range(4):
                at = depth * CELLS + pair * 128
                tile = value[:, at : at + 128]
                line = (2 * slab + depth) * 8 + 2 * pair
                flat[pl.ds(line, 8, stride=128), :] = tile
                flat[pl.ds(line + 1, 8, stride=128), :] = pltpu.roll(tile, 64, 1)
    o_ref[0] = flat[:, 0:64].reshape(8, 16, 8, 64).astype(BF)


def sum_and_spread(x_ref, o_ref):
    total = x_ref[0]
    for at in range(1, x_ref.shape[0]):
        total = total + x_ref[at]
    for at in range(o_ref.shape[0]):
        o_ref[at] = total


def unpack_gradients(core_ref, mine_ref, other_ref, one_ref, two_ref, both):
    core = core_ref[0]
    both[pl.ds(pl.multiple_of(core * HALF, HALF), HALF), :] = mine_ref[...]
    both[pl.ds(pl.multiple_of((1 - core) * HALF, HALF), HALF), :] = other_ref[...]
    two_ref[0:576, :] = both[0:576, 0:64]
    two_ref[576:1152, :] = both[0:576, 64:128]
    two_ref[1152:1440, :] = both[576:864, 0:64]
    two_ref[1440:1728, :] = both[576:864, 64:128]
    one_ref[0:432, :] = both[864:1296, 0:64]
    one_ref[432:864, :] = both[864:1296, 64:128]


def sds(shape, dtype):
    return jax.ShapeDtypeStruct(shape, dtype)


def with_core(kernel, outs, operands, scratch, flops, moved):
    whole = pl.BlockSpec(memory_space=pltpu.VMEM)
    return pl.pallas_call(
        kernel,
        in_specs=[pl.BlockSpec(memory_space=pltpu.SMEM)] + [whole] * operands,
        out_specs=[whole] * len(outs),
        out_shape=outs,
        scratch_shapes=scratch,
        compiler_params=pltpu.CompilerParams(vmem_limit_bytes=LIMIT),
        cost_estimate=pl.CostEstimate(flops=flops, bytes_accessed=moved, transcendentals=0),
    )


SPACE = ("y", "zh")
PLANE = ("x", "y")
LINE = ("zl", "zh")


def along(value, steps):
    count = lax.axis_size("y") * lax.axis_size("zh")
    pairs = [(at, at + steps) for at in range(count) if 0 <= at + steps < count]
    return lax.ppermute(value, SPACE, pairs)


def exchange(value, axes):
    return lax.all_to_all(value, axes, split_axis=0, concat_axis=0, tiled=True)


def shards(volumes, w_first, w_second, grad_out):
    core = lax.axis_index("core").astype(jnp.int32).reshape(1)
    kernel_one = w_first.reshape(27 * C0, C1)
    kernel_two = w_second.reshape(27 * C1, C1)
    lower = along(volumes[:, :, 3:], 1)
    packed = call(pack_cotangent, sds((8, 8, 2048), BF), [pltpu.VMEM((1024, 128), F)])(grad_out)
    cotangent = exchange(packed, SPACE).reshape(C1, 4 * CELLS)
    taps, spots, act, positive = call(
        first_block,
        [sds((27 * C0, SLAB), BF), sds((9 * C1, SLAB), BF), sds((C1, SLAB), BF), sds((C1, SLAB), BF)],
        [pltpu.VMEM((2048, 128), F), pltpu.VMEM((512, 128), F)],
    )(volumes, lower, kernel_one)
    below = along(act[:, CELLS:], 1)
    above = along(act[:, :CELLS], -1)
    mine, other = with_core(
        gradients,
        [sds((HALF, 128), F), sds((HALF, 128), F)],
        5,
        [pltpu.VMEM((3 * C1, SLAB), BF), pltpu.VMEM((ROWS, 128), F)],
        0,
        0,
    )(core, taps, spots, positive, cotangent, kernel_two)
    cores = lax.axis_size("core")
    pairs = [(at, at ^ 1) for at in range(cores)]
    chip = mine + lax.ppermute(other, "core", pairs)
    count = lax.axis_size("x") * lax.axis_size("y")
    deep = lax.axis_size("zl") * lax.axis_size("zh")
    share = HALF // count
    plane_parts = exchange(chip.reshape(count, share, 128), PLANE)
    line_in = call(sum_and_spread, sds((deep, share, 128), F))(plane_parts)
    line_parts = exchange(line_in, LINE)
    plane_in = call(sum_and_spread, sds((count, share, 128), F))(line_parts)
    my_half = exchange(plane_in, PLANE).reshape(HALF, 128)
    other_half = lax.ppermute(my_half, "core", pairs)
    total_one, total_two = with_core(
        unpack_gradients,
        [sds((27 * C0, C1), F), sds((27 * C1, C1), F)],
        2,
        [pltpu.VMEM((ROWS, 128), F)],
        0,
        0,
    )(core, my_half, other_half)
    own = call(second_block, sds((C1, SLAB), BF), [pltpu.VMEM((9 * C1, 4 * CELLS), BF)])(
        spots, below, above, kernel_two
    )
    gathered = exchange(own.reshape(8, 8, SLAB), SPACE)
    features = call(unpack_features, sds((1, 8, 16, 8, 64), BF), [pltpu.VMEM((1024, 128), F)])(gathered)
    return features, total_one.reshape(27, C0, C1), total_two.reshape(27, C1, C1)


def solution(mesh):
    fine = Mesh(np.asarray(mesh.devices).reshape(4, 4, 2, 4, 2), ("zl", "x", "core", "y", "zh"))
    dp, space = ("zl", "x", "core"), ("y", "zh")
    return jax.shard_map(
        shards,
        mesh=fine,
        in_specs=(P(dp, None, space, None, None), P(), P(), P(dp, space, None, None, None)),
        out_specs=(P(dp, space, None, None, None), P(), P()),
        check_vma=False,
    )
```

time: 552 us -> 121 us (0.22)
  waiting for transfers between devices: 361 us -> 8.35 us
  matrix products: 92.1 us -> 0 us
  blocking collectives: 0 us -> 58.7 us
  local copies, waits for them, and re-layouts: 63.1 us -> 6.06 us
  starting transfers between devices: 13.1 us -> 35.8 us
  between operations: 14.6 us -> 0.73 us
  Pallas kernels: 0 us -> 9.14 us
    psum x1 -> x0, waiting for transfers between devices: 259 us -> none  [shards(): lax.psum((whole_one.reshape(27, count_in, count_out), whole_two.reshape(2...]
    all_gather x2 -> x0, waiting for transfers between devices: 99.2 us -> none  [the longest x1 52 us: shards(): full_grad = lax.all_gather(grad_out, 'space', axis=1, tiled=True)]
    conv_general_dilated x5 -> x0, matrix products: 92.1 us -> none  [convolve(): lax.conv_general_dilated(lhs, rhs, (stride, stride, stride), pads, rhs_di...]
    all_to_all x0 -> x4, blocking collectives: none -> 58.7 us  [exchange(): return lax.all_to_all(value, axes, split_axis=0, concat_axis=0, tiled=True)]
    unnamed x32 -> x16, local copies, waits for them, and re-layouts: 28.1 us -> 5.14 us
    ppermute x1 -> x5, starting transfers between devices: 9.65 us -> 24.2 us  [the longest x3 16.5 us: along(): return lax.ppermute(value, SPACE, pairs)]
    all_gather x4 -> x0, local copies, waits for them, and re-layouts: 12.3 us -> none  [the longest x2 8.19 us: shards(): full_grad = lax.all_gather(grad_out, 'space', axis=1, tiled=True)]
    conv_general_dilated x8 -> x0, local copies, waits for them, and re-layouts: 10.3 us -> none  [convolve(): lax.conv_general_dilated(lhs, rhs, (stride, stride, stride), pads, rhs_di...]
  transfers between devices with their start and end apart: 5 -> 6, of which waited for: 4 -> 4; matrix products, arithmetic and copies ran while one was open for 19% -> 1% of each run, Pallas kernels for 0% -> 3%
where the time goes in v1:
time: 121 us; the launch traced here: 119 us
  blocking collectives  58.7 us (49%)
  starting transfers between devices  35.8 us (30%)
  Pallas kernels  9.14 us (8%)
  waiting for transfers between devices  8.35 us (7%)
  local copies, waits for them, and re-layouts  6.06 us (5%)
    all_to_all x4, blocking collectives, exchange(): return lax.all_to_all(value, axes, split_axis=0, concat_axis=0, tiled=True)  58.7 us
    ppermute x3, starting transfers between devices, along(): return lax.ppermute(value, SPACE, pairs)  16.5 us
    all_to_all x1, starting transfers between devices, exchange(): return lax.all_to_all(value, axes, split_axis=0, concat_axis=0, tiled=True)  11.6 us
    ppermute x3, waiting for transfers between devices, along(): return lax.ppermute(value, SPACE, pairs)  6.99 us
    unnamed x16, local copies, waits for them, and re-layouts  5.14 us
    ppermute x1, starting transfers between devices, shards(): other_half = lax.ppermute(my_half, 'core', pairs)  4.45 us
    ppermute x1, starting transfers between devices, shards(): chip = mine + lax.ppermute(other, 'core', pairs)  3.24 us
    pallas_call x1, Pallas kernels, shards(): with_core(gradients, [sds((HALF, 128), F), sds((HALF, 128), F)], 5, [pltp...  2.75 us
  transfers between devices with their start and end apart: 6, of which 4 were waited for; matrix products, arithmetic and copies ran while one was open for 1% of the time, Pallas kernels for 3%

profile of v1, /device:TPU:1, one launch (start us, length us, event | category | flops | bytes accessed | tf_op | source)
XLA Modules:
  0.0 118.8 jit_solution(17815153256176164639)
XLA Ops:
  0.6 0.0 copy-start.2
  0.6 0.9 copy-done.2
  1.6 1.0 shard_map.70
  2.6 11.6 %all-to-all-start.1 = ((bf16[8,8,2048]{2,1,0:T(8,128)(2,1)}), bf16[8,8,2048]{2,1,0:T(8,128)(2,1)}, u32[]{:S(2)}, u32[]{:S(2)}) async-start(bf16[8,8,2048]{2,1,0:T(8,128)(2,1)} %shard_map.70), calls=%async_computation.1 | async-start | bytes 524288 | tf_op jit(solution)/shard_map/all_to_all | solution.py:248
  14.3 0.9 slice.9
  15.2 7.3 %collective-permute-start = (bf16[1,32,1,16,128]{4,3,2,1,0:T(8,128)(2,1)S(1)}, bf16[1,32,1,16,128]{4,3,2,1,0:T(8,128)(2,1)S(1)}, u32[]{:S(2)}, u32[]{:S(2)}) collective-permute-start(bf16[1,32,1,16,128]{4,3,2,1,0:T(8,128)(2,1)S(1)} %slice.9), channel_id=1, source_target_pairs={{0,1},{1,2},{2,3},{3,4},{4,5},{5,6},{6,7},{8,9},{9,10},{10,11},{11... | collective-permute-start | bytes 393224 | tf_op jit(solution)/shard_map/ppermute | solution.py:244
  22.5 4.9 %collective-permute-done.h_ref = bf16[1,32,1,16,128]{4,3,2,1,0:T(8,128)(2,1)S(1)} collective-permute-done((bf16[1,32,1,16,128]{4,3,2,1,0:T(8,128)(2,1)S(1)}, bf16[1,32,1,16,128]{4,3,2,1,0:T(8,128)(2,1)S(1)}, u32[]{:S(2)}, u32[]{:S(2)}) %collective-permute-start) | collective-permute-done | bytes 131104 | tf_op jit(solution)/shard_map/ppermute | solution.py:244
  27.3 0.7 copy-done.6
  28.0 1.0 copy-done.1
  29.0 0.9 copy-done.3
  30.0 0.9 copy-done.7
  30.9 2.0 %shard_map.67 = (bf16[864,1024]{1,0:T(8,128)(2,1)S(1)}, bf16[576,1024]{1,0:T(8,128)(2,1)S(1)}, bf16[64,1024]{1,0:T(8,128)(2,1)S(1)}, bf16[64,1024]{1,0:T(8,128)(2,1)S(1)}) custom-call(bf16[1,32,4,16,128]{4,3,2,1,0:T(8,128)(2,1)S(1)} %copy-done.1, bf16[1,32,1,16,128]{4,3,2,1,0:T(8,128)(2,1)S(1)} %copy-done.7, bf16[864,64]{1,0:T(8,128)(2,1)S(1)} %bitcast.14), custom_call_target="tpu_custom_call" | custom-call | tf_op jit(solution)/shard_map/pallas_call | solution.py:258
  32.9 0.0 copy-start.4
  32.9 0.6 copy-done.4
  33.5 0.0 all-to-all-done.1
  33.5 2.8 %shard_map.71 = (f32[768,128]{1,0:T(8,128)S(1)}, f32[768,128]{1,0:T(8,128)S(1)}) custom-call(s32[1]{0:T(128)} %bitcast.3.core_ref, bf16[864,1024]{1,0:T(8,128)(2,1)S(1)} %get-tuple-element.13.u_ref, bf16[576,1024]{1,0:T(8,128)(2,1)S(1)} %get-tuple-element.11.x_ref, bf16[64,1024]{1,0:T(8,128)(2,1)S(1)} %get-tuple-element.14.pos_ref, ...), custom_call_target="tpu_custom_call" | custom-call | tf_op jit(solution)/shard_map/pallas_call | solution.py:265
  36.3 3.2 %collective-permute-start.3 = (f32[768,128]{1,0:T(8,128)S(1)}, f32[768,128]{1,0:T(8,128)S(1)}, u32[]{:S(2)}, u32[]{:S(2)}) collective-permute-start(f32[768,128]{1,0:T(8,128)S(1)} %get-tuple-element.16), channel_id=1, source_target_pairs={{0,8},{8,0},{1,9},{9,1},{2,10},{10,2},{3,11},{11,3},{4,12},{12,4},... | collective-permute-start | bytes 1179656 | tf_op jit(solution)/shard_map/ppermute | solution.py:275
  39.5 1.3 %collective-permute-done.3 = f32[768,128]{1,0:T(8,128)S(1)} collective-permute-done((f32[768,128]{1,0:T(8,128)S(1)}, f32[768,128]{1,0:T(8,128)S(1)}, u32[]{:S(2)}, u32[]{:S(2)}) %collective-permute-start.3) | collective-permute-done | bytes 393248 | tf_op jit(solution)/shard_map/ppermute | solution.py:275
  40.9 0.0 copy-start.5
  41.0 16.9 %all_to_all.25.x_ref = f32[16,48,128]{2,1,0:T(8,128)S(1)} all-to-all(f32[16,48,128]{2,1,0:T(8,128)S(1)} %bitcast.15), channel_id=1, replica_groups=mesh['zl'=4,'x'=4,'core'=2,'y'=4,'zh'=2] {'x','y'}, dimensions={0} | all-to-all | bytes 786432 | tf_op jit(solution)/shard_map/all_to_all | solution.py:248
  57.9 13.0 %all_to_all.26.x_ref = f32[8,48,128]{2,1,0:T(8,128)S(1)} all-to-all(f32[8,48,128]{2,1,0:T(8,128)S(1)} %shard_map.72), channel_id=1, replica_groups=mesh['zl'=4,'x'=4,'core'=2,'y'=4,'zh'=2] {'zl','zh'}, dimensions={0} | all-to-all | bytes 393216 | tf_op jit(solution)/shard_map/all_to_all | solution.py:248
  70.9 11.3 %all_to_all.27 = f32[16,48,128]{2,1,0:T(8,128)S(1)} all-to-all(f32[16,48,128]{2,1,0:T(8,128)S(1)} %shard_map.73), channel_id=1, replica_groups=mesh['zl'=4,'x'=4,'core'=2,'y'=4,'zh'=2] {'x','y'}, dimensions={0} | all-to-all | bytes 786432 | tf_op jit(solution)/shard_map/all_to_all | solution.py:248
  82.2 4.4 %collective-permute-start.4 = (f32[768,128]{1,0:T(8,128)S(1)}, f32[768,128]{1,0:T(8,128)S(1)}, u32[]{:S(2)}, u32[]{:S(2)}) collective-permute-start(f32[768,128]{1,0:T(8,128)S(1)} %bitcast.11), channel_id=1, source_target_pairs={{0,8},{8,0},{1,9},{9,1},{2,10},{10,2},{3,11},{11,3},{4,12},{12,4},... | collective-permute-start | bytes 1179656 | tf_op jit(solution)/shard_map/ppermute | solution.py:284
  86.7 1.3 %collective-permute-start.2 = (bf16[64,512]{1,0:T(8,128)(2,1)S(1)}, bf16[64,512]{1,0:T(8,128)(2,1)S(1)}, u32[]{:S(2)}, u32[]{:S(2)}) collective-permute-start(bf16[64,512]{1,0:T(8,128)(2,1)S(1)} %get-tuple-element.19), channel_id=1, source_target_pairs={{1,0},{2,1},{3,2},{4,3},{5,4},{6,5},{7,6},{9,8},{10,9},{11,10},{12... | collective-permute-start | bytes 196616 | tf_op jit(solution)/shard_map/ppermute | solution.py:244
  88.0 7.9 %collective-permute-start.1 = (bf16[64,512]{1,0:T(8,128)(2,1)S(1)}, bf16[64,512]{1,0:T(8,128)(2,1)S(1)}, u32[]{:S(2)}, u32[]{:S(2)}) collective-permute-start(bf16[64,512]{1,0:T(8,128)(2,1)S(1)} %get-tuple-element.20), channel_id=1, source_target_pairs={{0,1},{1,2},{2,3},{3,4},{4,5},{5,6},{6,7},{8,9},{9,10},{10,11},{11... | collective-permute-start | bytes 196616 | tf_op jit(solution)/shard_map/ppermute | solution.py:244
  95.9 0.3 collective-permute-done.2.above_ref
  96.2 1.8 %collective-permute-done.1.below_ref = bf16[64,512]{1,0:T(8,128)(2,1)S(1)} collective-permute-done((bf16[64,512]{1,0:T(8,128)(2,1)S(1)}, bf16[64,512]{1,0:T(8,128)(2,1)S(1)}, u32[]{:S(2)}, u32[]{:S(2)}) %collective-permute-start.1) | collective-permute-done | bytes 65568 | tf_op jit(solution)/shard_map/ppermute | solution.py:244
  98.0 0.9 shard_map.68
  98.9 17.5 %all_to_all.28.x_ref = bf16[8,8,1024]{2,1,0:T(8,128)(2,1)S(1)} all-to-all(bf16[8,8,1024]{2,1,0:T(8,128)(2,1)S(1)} %bitcast.13), channel_id=1, replica_groups=mesh['zl'=4,'x'=4,'core'=2,'y'=4,'zh'=2] {'y','zh'}, dimensions={0} | all-to-all | bytes 262144 | tf_op jit(solution)/shard_map/all_to_all | solution.py:248
  116.5 1.1 shard_map.69
  117.5 0.0 collective-permute-done.4.other_ref
  117.5 1.3 %shard_map.74 = (f32[864,64]{1,0:T(8,128)}, f32[1728,64]{1,0:T(8,128)}) custom-call(s32[1]{0:T(128)} %bitcast.3.core_ref, f32[768,128]{1,0:T(8,128)S(1)} %bitcast.12, f32[768,128]{1,0:T(8,128)S(1)} %collective-permute-done.4.other_ref), custom_call_target="tpu_custom_call" | custom-call | tf_op jit(solution)/shard_map/pallas_call | solution.py:285
  (11 shorter events, 0.1 us)
Async XLA Ops:
  0.6 1.0 copy-start.2
  1.6 32.0 %copy-start = (bf16[27,64,64]{2,1,0:T(8,128)(2,1)S(1)}, bf16[27,64,64]{2,1,0:T(8,128)(2,1)}, u32[]{:S(2)}) copy-start(bf16[27,64,64]{2,1,0:T(8,128)(2,1)} %param.6) | copy-start | bytes 663556
  2.6 30.9 %all-to-all-start.1 = ((bf16[8,8,2048]{2,1,0:T(8,128)(2,1)}), bf16[8,8,2048]{2,1,0:T(8,128)(2,1)}, u32[]{:S(2)}, u32[]{:S(2)}) async-start(bf16[8,8,2048]{2,1,0:T(8,128)(2,1)} %shard_map.70), calls=%async_computation.1 | async-start | bytes 524288 | tf_op jit(solution)/shard_map/all_to_all | solution.py:248
  15.2 12.1 %collective-permute-start = (bf16[1,32,1,16,128]{4,3,2,1,0:T(8,128)(2,1)S(1)}, bf16[1,32,1,16,128]{4,3,2,1,0:T(8,128)(2,1)S(1)}, u32[]{:S(2)}, u32[]{:S(2)}) collective-permute-start(bf16[1,32,1,16,128]{4,3,2,1,0:T(8,128)(2,1)S(1)} %slice.9), channel_id=1, source_target_pairs={{0,1},{1,2},{2,3},{3,4},{4,5},{5,6},{6,7},{8,9},{9,10},{10,11},{11... | collective-permute-start | bytes 393224 | tf_op jit(solution)/shard_map/ppermute | solution.py:244
  27.3 0.7 copy-start.6
  28.0 1.0 copy-start.1
  29.0 0.9 copy-start.3
  30.0 0.9 copy-start.7
  32.9 0.7 copy-start.4
  36.3 4.6 %collective-permute-start.3 = (f32[768,128]{1,0:T(8,128)S(1)}, f32[768,128]{1,0:T(8,128)S(1)}, u32[]{:S(2)}, u32[]{:S(2)}) collective-permute-start(f32[768,128]{1,0:T(8,128)S(1)} %get-tuple-element.16), channel_id=1, source_target_pairs={{0,8},{8,0},{1,9},{9,1},{2,10},{10,2},{3,11},{11,3},{4,12},{12,4},... | collective-permute-start | bytes 1179656 | tf_op jit(solution)/shard_map/ppermute | solution.py:275
  40.9 45.7 %copy-start.5 = (bf16[64,1024]{1,0:T(8,128)(2,1)S(1)}, bf16[64,1024]{1,0:T(8,128)(2,1)}, u32[]{:S(2)}) copy-start(bf16[64,1024]{1,0:T(8,128)(2,1)} %copy-done.4) | copy-start | bytes 393220
  82.2 35.4 %collective-permute-start.4 = (f32[768,128]{1,0:T(8,128)S(1)}, f32[768,128]{1,0:T(8,128)S(1)}, u32[]{:S(2)}, u32[]{:S(2)}) collective-permute-start(f32[768,128]{1,0:T(8,128)S(1)} %bitcast.11), channel_id=1, source_target_pairs={{0,8},{8,0},{1,9},{9,1},{2,10},{10,2},{3,11},{11,3},{4,12},{12,4},... | collective-permute-start | bytes 1179656 | tf_op jit(solution)/shard_map/ppermute | solution.py:284
  86.7 9.5 %collective-permute-start.2 = (bf16[64,512]{1,0:T(8,128)(2,1)S(1)}, bf16[64,512]{1,0:T(8,128)(2,1)S(1)}, u32[]{:S(2)}, u32[]{:S(2)}) collective-permute-start(bf16[64,512]{1,0:T(8,128)(2,1)S(1)} %get-tuple-element.19), channel_id=1, source_target_pairs={{1,0},{2,1},{3,2},{4,3},{5,4},{6,5},{7,6},{9,8},{10,9},{11,10},{12... | collective-permute-start | bytes 196616 | tf_op jit(solution)/shard_map/ppermute | solution.py:244
  88.0 10.0 %collective-permute-start.1 = (bf16[64,512]{1,0:T(8,128)(2,1)S(1)}, bf16[64,512]{1,0:T(8,128)(2,1)S(1)}, u32[]{:S(2)}, u32[]{:S(2)}) collective-permute-start(bf16[64,512]{1,0:T(8,128)(2,1)S(1)} %get-tuple-element.20), channel_id=1, source_target_pairs={{0,1},{1,2},{2,3},{3,4},{4,5},{5,6},{6,7},{8,9},{9,10},{10,11},{11... | collective-permute-start | bytes 196616 | tf_op jit(solution)/shard_map/ppermute | solution.py:244

commit v2 on v1

v2 whole, which is shorter than its diff:
```python
import jax
import jax.numpy as jnp
import numpy as np
from jax import lax
from jax.experimental import pallas as pl
from jax.experimental.pallas import tpu as pltpu
from jax.sharding import Mesh, PartitionSpec as P

SLOPE = 0.3
BF = jnp.bfloat16
F = jnp.float32
COST_PACK = 4000000
COST_FIRST = 8000000
FLOPS_FIRST = 10000000000
FLOPS_GRAD = 0
FLOPS_LAST = 2000000000
COST_OWN = 12000000
COST_GRAD = 12000000
SENT = BF
C0, C1 = 32, 64
CELLS = 512
SLAB = 2 * CELLS
ROWS = 1536
HALF = ROWS // 2
LIMIT = 8 * 1024 * 1024


def call(kernel, outs, scratch=(), flops=0, moved=0, limit=LIMIT, **spec):
    return pl.pallas_call(
        kernel,
        **spec,
        out_shape=outs,
        scratch_shapes=list(scratch),
        compiler_params=pltpu.CompilerParams(vmem_limit_bytes=limit),
        cost_estimate=pl.CostEstimate(flops=flops, bytes_accessed=moved, transcendentals=0),
    )


def lanes(shape):
    return lax.broadcasted_iota(jnp.int32, shape, 1)


def low_half(shape):
    return lanes(shape) < 64


def cell_index(shape):
    lane = lanes(shape)
    return (lane // 64) % 8, lane % 64


def shifted(value, row, rows, col, cols):
    width = value.shape[1]
    moved = pltpu.roll(value, (-(64 * rows + cols)) % width, 1)
    inside = (row + rows >= 0) & (row + rows < 8) & (col + cols >= 0) & (col + cols < 64)
    return jnp.where(inside, moved, 0.0)


def nine_shifts(act, store):
    row, col = cell_index(act.shape)
    for c in range(3):
        side = act if c == 1 else shifted(act, row, 0, col, c - 1)
        for b in range(3):
            store(3 * b + c, side if b == 1 else shifted(side, row, b - 1, col, 0))


def shift_all(act, target):
    def store(offset, value):
        target[offset * C1 : (offset + 1) * C1, :] = value.astype(BF)

    nine_shifts(act.astype(F), store)


def pack_inputs(x_ref, v_ref, o_ref, last_ref, held, flat, sems):
    load = pltpu.make_async_copy(x_ref.at[0], held, sems.at[0])
    plane_copy = pltpu.make_async_copy(v_ref.at[:, :, 3:4], last_ref, sems.at[1])
    load.start()
    plane_copy.start()
    load.wait()
    flat[:, 0:64] = held[...].astype(F).reshape(1024, 64)
    low = low_half((8, 128))
    zero = jnp.zeros((8, CELLS), BF)
    o_ref[0, :, 0:CELLS] = zero
    o_ref[7, :, 3 * CELLS :] = zero
    for plane in range(16):
        tiles = []
        for pair in range(4):
            first = flat[pl.ds(plane * 8 + 2 * pair, 8, stride=128), :]
            second = flat[pl.ds(plane * 8 + 2 * pair + 1, 8, stride=128), :]
            tiles.append(jnp.where(low, first, pltpu.roll(second, 64, 1)))
        value = jnp.concatenate(tiles, axis=1).astype(BF)
        for slab in range(8):
            slot = plane - 2 * slab + 1
            if 0 <= slot < 4:
                o_ref[slab, :, slot * CELLS : (slot + 1) * CELLS] = value
    plane_copy.wait()


def deinterleave(lines, row, col):
    low = low_half((C0, 128))
    phase = {}
    for odd in range(2):
        even_cols, odd_cols = [], []
        for pair in range(4):
            first, second = lines(4 * pair + odd), lines(4 * pair + 2 + odd)
            even_cols.append(jnp.where(low, first, pltpu.roll(second, 64, 1)))
            odd_cols.append(jnp.where(low, pltpu.roll(first, 64, 1), second))
        phase[odd, 0] = jnp.concatenate(even_cols, axis=1)
        phase[odd, 1] = jnp.concatenate(odd_cols, axis=1)
    left = [shifted(phase[odd, 1], row, 0, col, -1) for odd in range(2)]
    taps = {
        (1, 1): phase[0, 0],
        (1, 2): phase[0, 1],
        (1, 0): left[0],
        (2, 1): phase[1, 0],
        (2, 2): phase[1, 1],
        (2, 0): left[1],
        (0, 1): shifted(phase[1, 0], row, -1, col, 0),
        (0, 2): shifted(phase[1, 1], row, -1, col, 0),
        (0, 0): shifted(left[1], row, -1, col, 0),
    }
    return [((3 * b + c) * C0, value.astype(BF)) for (b, c), value in taps.items()]


def column_split():
    source = lax.broadcasted_iota(jnp.int32, (128, 128), 0)
    target = lanes((128, 128))
    pick = jnp.where(target < 64, 2 * target, 2 * target - 127)
    return (source == pick).astype(F).astype(BF)


def own_taps(v_ref, w_ref, k_ref, zero_ref, rest_ref, one_ref, two_ref, own):
    own[...] = jnp.dot(v_ref[0].reshape(2048, 128), column_split(), preferred_element_type=F)
    row, col = cell_index((C0, CELLS))
    for plane in range(1, 5):
        base = (plane - 1) * 16
        for at, value in deinterleave(lambda line: own[pl.ds(base + line, C0, stride=64), :], row, col):
            for depth in range(2):
                a = plane - 2 * depth
                if a == 0:
                    zero_ref[at : at + C0, :] = value
                if 1 <= a < 3:
                    start = (a - 1) * 9 * C0 + at
                    rest_ref[start : start + C0, depth * CELLS : (depth + 1) * CELLS] = value
    one_ref[...] = w_ref[...]
    two_ref[...] = jnp.concatenate([k_ref[a * 576 : (a + 1) * 576, :] for a in range(3)], axis=1)


def first_block(at_ref, h_ref, zero_ref, rest_ref, one_ref, two_ref, u_ref, act_ref, keep_ref, send_ref, halo, spots, parts):
    halo[...] = jnp.dot(h_ref[0].reshape(512, 128), column_split(), preferred_element_type=F)
    row, col = cell_index((C0, CELLS))
    for at, value in deinterleave(lambda line: halo[pl.ds(line, C0, stride=16), :], row, col):
        u_ref[at : at + C0, :] = value
    down = (((0,), (0,)), ((), ()))
    pre = lax.dot_general(one_ref[9 * C0 :, :], rest_ref[...], down, preferred_element_type=F)
    outer = jnp.concatenate([u_ref[...], zero_ref[...]], axis=1)
    pre = pre + lax.dot_general(one_ref[: 9 * C0, :], outer, down, preferred_element_type=F)
    act = jnp.where(pre > 0, pre, SLOPE * pre).astype(BF)
    act_ref[...] = act
    shift_all(act, spots)
    sums = lax.dot_general(two_ref[...], spots[...], down, preferred_element_type=F)
    early, late = sums[:, :CELLS], sums[:, CELLS:]
    back, same, ahead = (slice(a * C1, (a + 1) * C1) for a in range(3))
    slots = (early[ahead], early[same] + late[ahead], early[back] + late[same], late[back])
    for slot, value in enumerate(slots):
        parts[:, slot * CELLS : (slot + 1) * CELLS] = value
    side = at_ref[1]
    for group in range(4):
        own = pl.multiple_of(group * 16 + side * 8, 8)
        other = pl.multiple_of(group * 16 + (1 - side) * 8, 8)
        keep_ref[group] = parts[pl.ds(own, 8), :]
        send_ref[group] = parts[pl.ds(other, 8), :].astype(BF)


def gradients(at_ref, u_ref, zero_ref, rest_ref, act_ref, g_ref, two_ref, mine_ref, other_ref, depths, spots, both):
    for a in range(3):
        depths[a * C1 : (a + 1) * C1, :] = g_ref[:, (2 - a) * CELLS : (2 - a) * CELLS + SLAB]
    shape = (C1, SLAB)
    row, col = cell_index(shape)
    spread = jnp.dot(two_ref[...], depths[...], preferred_element_type=F)
    total = None
    for c in range(3):
        side = None
        for b in range(3):
            at = (3 * b + c) * C1
            part = spread[at : at + C1, :]
            part = part if b == 1 else shifted(part, row, 1 - b, col, 0)
            side = part if side is None else side + part
        side = side if c == 1 else shifted(side, row, 0, col, 1 - c)
        total = side if total is None else total + side
    grad_act = total.astype(BF).astype(F)
    act = act_ref[...].astype(F)
    grad_pre = (grad_act * jnp.where(act > 0, 1.0, SLOPE)).astype(BF)
    shift_all(act, spots)
    across = (((1,), (1,)), ((), ()))
    second = lax.dot_general(spots[...], depths[...], across, preferred_element_type=F)
    outer = jnp.concatenate([u_ref[...], zero_ref[...]], axis=1)
    first = lax.dot_general(outer, grad_pre, across, preferred_element_type=F)
    rest = lax.dot_general(rest_ref[...], grad_pre, across, preferred_element_type=F)
    both[0:576, :] = second[:, 0:128]
    both[576:864, :] = jnp.concatenate([second[0:288, 128:192], second[288:576, 128:192]], axis=1)
    both[864:1008, :] = jnp.concatenate([first[0:144, :], first[144:288, :]], axis=1)
    both[1008:1296, :] = jnp.concatenate([rest[0:288, :], rest[288:576, :]], axis=1)
    both[1296:ROWS, :] = jnp.zeros((ROWS - 1296, 128), F)
    core = at_ref[0]
    mine_ref[...] = both[pl.ds(pl.multiple_of(core * HALF, HALF), HALF), :]
    other_ref[...] = both[pl.ds(pl.multiple_of((1 - core) * HALF, HALF), HALF), :]


def join_sides(at_ref, keep_ref, got_ref, *o_refs):
    lower = at_ref[1] == 0
    for step, o_ref in enumerate(o_refs):
        group = lax.rem(at_ref[2] + step, 4)
        kept, got = keep_ref[group], got_ref[group].astype(F)
        first, second = jnp.where(lower, kept, got), jnp.where(lower, got, kept)
        middle = first[:, 2 * CELLS :] + second[:, : 2 * CELLS]
        joined = jnp.concatenate([first[:, : 2 * CELLS], middle, second[:, 2 * CELLS :]], axis=1)
        o_ref[...] = joined.astype(o_ref.dtype)


def unpack_features(at_ref, own_ref, one_ref, two_ref, three_ref, o_ref, groups, flat):
    for step, ref in enumerate((own_ref, one_ref, two_ref, three_ref)):
        groups[lax.rem(at_ref[2] + 4 - step, 4)] = ref[...].astype(F)
    for plane in range(16):
        group, at = plane // 4, plane % 4 + 1
        value = groups[group, :, at * CELLS : (at + 1) * CELLS]
        near, slot = {1: (group - 1, 5), 4: (group + 1, 0)}.get(at, (-1, 0))
        if 0 <= near < 4:
            value = value + groups[near, :, slot * CELLS : (slot + 1) * CELLS]
        for pair in range(4):
            tile = value[:, pair * 128 : (pair + 1) * 128]
            line = plane * 8 + 2 * pair
            flat[pl.ds(line, 8, stride=128), :] = tile
            flat[pl.ds(line + 1, 8, stride=128), :] = pltpu.roll(tile, 64, 1)
    o_ref[0] = flat[:, 0:64].reshape(8, 16, 8, 64).astype(BF)


def sum_and_spread(x_ref, o_ref):
    total = x_ref[0].astype(F)
    for at in range(1, x_ref.shape[0]):
        total = total + x_ref[at].astype(F)
    total = total.astype(o_ref.dtype)
    for at in range(o_ref.shape[0]):
        o_ref[at] = total


def unpack_gradients(at_ref, mine_ref, other_ref, one_ref, two_ref, both):
    core = at_ref[0]
    both[pl.ds(pl.multiple_of(core * HALF, HALF), HALF), :] = mine_ref[...].astype(F)
    both[pl.ds(pl.multiple_of((1 - core) * HALF, HALF), HALF), :] = other_ref[...].astype(F)
    two_ref[0:576, :] = both[0:576, 0:64]
    two_ref[576:1152, :] = both[0:576, 64:128]
    two_ref[1152:1440, :] = both[576:864, 0:64]
    two_ref[1440:1728, :] = both[576:864, 64:128]
    one_ref[0:144, :] = both[864:1008, 0:64]
    one_ref[144:288, :] = both[864:1008, 64:128]
    one_ref[288:576, :] = both[1008:1296, 0:64]
    one_ref[576:864, :] = both[1008:1296, 64:128]


def sds(shape, dtype):
    return jax.ShapeDtypeStruct(shape, dtype)


def with_place(kernel, outs, operands, scratch, flops, moved):
    whole = pl.BlockSpec(memory_space=pltpu.VMEM)
    return pl.pallas_call(
        kernel,
        in_specs=[pl.BlockSpec(memory_space=pltpu.SMEM)] + [whole] * operands,
        out_specs=[whole] * len(outs),
        out_shape=outs,
        scratch_shapes=scratch,
        compiler_params=pltpu.CompilerParams(vmem_limit_bytes=LIMIT),
        cost_estimate=pl.CostEstimate(flops=flops, bytes_accessed=moved, transcendentals=0),
    )


SPACE = ("y", "zh")
PLANE = ("x", "y")
LINE = ("zl", "zh")


def along(value, steps):
    count = lax.axis_size("y") * lax.axis_size("zh")
    pairs = [(at, at + steps) for at in range(count) if 0 <= at + steps < count]
    return lax.ppermute(value, SPACE, pairs)


def exchange(value, axes):
    return lax.all_to_all(value, axes, split_axis=0, concat_axis=0, tiled=True)


def shards(volumes, w_first, w_second, grad_out):
    place = jnp.stack([lax.axis_index("core"), lax.axis_index("zh"), lax.axis_index("y")]).astype(jnp.int32)
    kernel_one = w_first.reshape(27 * C0, C1)
    kernel_two = w_second.reshape(27 * C1, C1)
    far = pl.BlockSpec(memory_space=pltpu.HBM)
    near = pl.BlockSpec(memory_space=pltpu.VMEM)
    packed, last = call(
        pack_inputs,
        [sds((8, 8, 2048), BF), sds((1, C0, 1, 16, 128), BF)],
        [pltpu.VMEM((8, 16, 8, 64), BF), pltpu.VMEM((1024, 128), F), pltpu.SemaphoreType.DMA((2,))],
        0,
        COST_PACK,
        60 * 1024 * 1024,
        in_specs=[far, far],
        out_specs=[near, near],
    )(grad_out, volumes)
    lower = along(last, 1)
    cotangent = exchange(packed, SPACE).reshape(C1, 4 * CELLS)
    zero, rest, one, two = call(
        own_taps,
        [sds((9 * C0, CELLS), BF), sds((18 * C0, SLAB), BF), sds((27 * C0, C1), BF), sds((9 * C1, 3 * C1), BF)],
        [pltpu.VMEM((2048, 128), F)],
        0,
        COST_OWN,
    )(volumes, kernel_one, kernel_two)
    taps, act, keep, send = with_place(
        first_block,
        [sds((9 * C0, CELLS), BF), sds((C1, SLAB), BF), sds((4, 8, 4 * CELLS), F), sds((4, 8, 4 * CELLS), BF)],
        5,
        [pltpu.VMEM((512, 128), F), pltpu.VMEM((9 * C1, SLAB), BF), pltpu.VMEM((C1, 4 * CELLS), F)],
        FLOPS_FIRST,
        COST_FIRST,
    )(place, lower, zero, rest, one, two)
    got = lax.ppermute(send, "zh", [(0, 1), (1, 0)])
    mine, other = with_place(
        gradients,
        [sds((HALF, 128), F), sds((HALF, 128), F)],
        6,
        [pltpu.VMEM((3 * C1, SLAB), BF), pltpu.VMEM((9 * C1, SLAB), BF), pltpu.VMEM((ROWS, 128), F)],
        FLOPS_GRAD,
        COST_GRAD,
    )(place, taps, zero, rest, act, cotangent, two)
    cores = lax.axis_size("core")
    pairs = [(at, at ^ 1) for at in range(cores)]
    other, got = lax.optimization_barrier((other, got))
    side = (8, 6 * CELLS)
    joined = with_place(join_sides, [sds(side, F)] + [sds(side, BF)] * 3, 2, [], 0, 10000)(place, keep, got)
    chip = mine + lax.ppermute(other, "core", pairs)
    chip, joined = lax.optimization_barrier((chip.astype(SENT), joined))
    count = lax.axis_size("x") * lax.axis_size("y")
    deep = lax.axis_size("zl") * lax.axis_size("zh")
    share = HALF // count
    plane_parts = exchange(chip.reshape(count, share, 128), PLANE)
    line_in = call(sum_and_spread, sds((deep, share, 128), SENT), (), 0, 10000)(plane_parts)
    line_parts = exchange(line_in, LINE)
    moved = [
        lax.ppermute(joined[step], "y", [(at, (at + step) % 4) for at in range(4)]) for step in range(1, 4)
    ]
    plane_in = call(sum_and_spread, sds((count, share, 128), SENT), (), 0, 10000)(line_parts)
    plane_in, moved = lax.optimization_barrier((plane_in, moved))
    my_half = exchange(plane_in, PLANE).reshape(HALF, 128)
    other_half = lax.ppermute(my_half, "core", pairs)
    total_one, total_two = with_place(
        unpack_gradients,
        [sds((27 * C0, C1), F), sds((27 * C1, C1), F)],
        2,
        [pltpu.VMEM((ROWS, 128), F)],
        FLOPS_LAST,
        4000000,
    )(place, my_half, other_half)
    features = with_place(
        unpack_features,
        [sds((1, 8, 16, 8, 64), BF)],
        4,
        [pltpu.VMEM((4,) + side, F), pltpu.VMEM((1024, 128), F)],
        0,
        10000,
    )(place, joined[0], *moved)[0]
    return features, total_one.reshape(27, C0, C1), total_two.reshape(27, C1, C1)


def solution(mesh):
    fine = Mesh(np.asarray(mesh.devices).reshape(4, 4, 2, 4, 2), ("zl", "x", "core", "y", "zh"))
    dp, space = ("zl", "x", "core"), ("y", "zh")
    return jax.shard_map(
        shards,
        mesh=fine,
        in_specs=(P(dp, None, space, None, None), P(), P(), P(dp, space, None, None, None)),
        out_specs=(P(dp, space, None, None, None), P(), P()),
        check_vma=False,
    )
```

time: 121 us -> 81.5 us (0.67); the launches traced: 119 us -> 81.1 us
  blocking collectives: 58.7 us -> 25.2 us
  local copies, waits for them, and re-layouts: 6.06 us -> 0.01 us
  Pallas kernels: 9.14 us -> 13 us
    all_to_all x4 -> x2, blocking collectives: 58.7 us -> 25.2 us  [exchange(): return lax.all_to_all(value, axes, split_axis=0, concat_axis=0, tiled=True)]
    ppermute x0 -> x4, starting transfers between devices: none -> 8.99 us  [the longest x1 5.44 us: shards(): got = lax.ppermute(send, 'zh', [(0, 1), (1, 0)])]
    ppermute x3 -> x1, waiting for transfers between devices: 6.99 us -> 0.01 us  [along(): return lax.ppermute(value, SPACE, pairs)]
    ppermute x3 -> x1, starting transfers between devices: 16.5 us -> 9.65 us  [along(): return lax.ppermute(value, SPACE, pairs)]
    all_to_all x1 -> x2, waiting for transfers between devices: 0.01 us -> 5.26 us  [exchange(): return lax.all_to_all(value, axes, split_axis=0, concat_axis=0, tiled=True)]
    unnamed x16 -> x6, local copies, waits for them, and re-layouts: 5.14 us -> 0.01 us
    pallas_call x8 -> x9, Pallas kernels: 9.14 us -> 13 us  [the longest x1 2.53 us: shards(): with_place(gradients, [sds((HALF, 128), F), sds((HALF, 128), F)], 6, [plt...]
    ppermute x1, starting transfers between devices: 3.24 us -> 0.77 us  [shards(): chip = mine + lax.ppermute(other, 'core', pairs)]
  transfers between devices with their start and end apart: 6 -> 9, of which waited for: 4 -> 4; matrix products, arithmetic and copies ran while one was open for 1% -> 0% of each run, Pallas kernels for 3% -> 10%
where the time goes in v2:
time: 81.5 us; the launch traced here: 81.1 us
  starting transfers between devices  34.6 us (42%)
  blocking collectives  25.2 us (31%)
  Pallas kernels  13 us (16%)
  waiting for transfers between devices  7.38 us (9%)
    all_to_all x2, blocking collectives, exchange(): return lax.all_to_all(value, axes, split_axis=0, concat_axis=0, tiled=True)  25.2 us
    all_to_all x2, starting transfers between devices, exchange(): return lax.all_to_all(value, axes, split_axis=0, concat_axis=0, tiled=True)  10.8 us
    ppermute x1, starting transfers between devices, along(): return lax.ppermute(value, SPACE, pairs)  9.65 us
    ppermute x1, starting transfers between devices, shards(): got = lax.ppermute(send, 'zh', [(0, 1), (1, 0)])  5.44 us
    all_to_all x2, waiting for transfers between devices, exchange(): return lax.all_to_all(value, axes, split_axis=0, concat_axis=0, tiled=True)  5.26 us
    ppermute x1, starting transfers between devices, shards(): other_half = lax.ppermute(my_half, 'core', pairs)  4.41 us
    ppermute x3, starting transfers between devices, shards(): lax.ppermute(joined[step], 'y', [(at, (at + step) % 4) for at in range(4)])  3.55 us
    pallas_call x1, Pallas kernels, shards(): with_place(gradients, [sds((HALF, 128), F), sds((HALF, 128), F)], 6, [plt...  2.53 us
  transfers between devices with their start and end apart: 9, of which 4 were waited for; matrix products, arithmetic and copies ran while one was open for 0% of the time, Pallas kernels for 10%

profile of v2, /device:TPU:1, one launch (start us, length us, event | category | flops | bytes accessed | tf_op | source)
XLA Modules:
  0.0 81.1 jit_solution(13007478721711325584)
XLA Ops:
  0.6 0.0 copy-start
  0.6 0.0 copy-start.1
  0.7 0.0 copy-start.2
  0.7 2.1 %shard_map.67 = (bf16[8,8,2048]{2,1,0:T(8,128)(2,1)}, bf16[1,32,1,16,128]{4,3,2,1,0:T(8,128)(2,1)}) custom-call(bf16[1,8,16,8,64]{4,3,2,1,0:T(8,128)(2,1)} %x_ref.1, bf16[1,32,4,16,128]{4,3,2,1,0:T(8,128)(2,1)} %v_ref.3), custom_call_target="tpu_custom_call" | custom-call | bytes 4000000 | tf_op jit(solution)/shard_map/pallas_call | solution.py:299
  2.8 9.6 %collective-permute-start = (bf16[1,32,1,16,128]{4,3,2,1,0:T(8,128)(2,1)}, bf16[1,32,1,16,128]{4,3,2,1,0:T(8,128)(2,1)S(1)}, u32[]{:S(2)}, u32[]{:S(2)}) collective-permute-start(bf16[1,32,1,16,128]{4,3,2,1,0:T(8,128)(2,1)} %get-tuple-element.32), channel_id=1, source_target_pairs={{0,1},{1,2},{2,3},{3,4},{4,5},{5,6},{6,7},{8,9},{9,10},{10,11},{11... | collective-permute-start | bytes 393224 | tf_op jit(solution)/shard_map/ppermute | solution.py:286
  12.4 4.2 %all-to-all-start = ((bf16[8,8,2048]{2,1,0:T(8,128)(2,1)}), bf16[8,8,2048]{2,1,0:T(8,128)(2,1)S(1)}, u32[]{:S(2)}, u32[]{:S(2)}) async-start(bf16[8,8,2048]{2,1,0:T(8,128)(2,1)} %get-tuple-element.39), calls=%async_computation | async-start | bytes 524288 | tf_op jit(solution)/shard_map/all_to_all | solution.py:290
  16.7 1.3 %shard_map.68 = (bf16[288,512]{1,0:T(8,128)(2,1)S(1)}, bf16[576,1024]{1,0:T(8,128)(2,1)S(1)}, bf16[864,64]{1,0:T(8,128)(2,1)S(1)}, bf16[576,192]{1,0:T(8,128)(2,1)S(1)}) custom-call(bf16[1,32,4,16,128]{4,3,2,1,0:T(8,128)(2,1)S(1)} %copy-done, bf16[864,64]{1,0:T(8,128)(2,1)S(1)} %bitcast.12, bf16[1728,64]{1,0:T(8,128)(2,1)S(1)} %bitcast.11), custom_call_target="tpu_custom_call" | custom-call | bytes 12000000 | tf_op jit(solution)/shard_map/pallas_call | solution.py:311
  18.0 0.1 pad_add_fusion.at_ref
  18.1 0.0 collective-permute-done.h_ref
  18.1 2.2 %shard_map.69 = (bf16[288,512]{1,0:T(8,128)(2,1)S(1)}, bf16[64,1024]{1,0:T(8,128)(2,1)S(1)}, f32[4,8,2048]{2,1,0:T(8,128)S(1)}, bf16[4,8,2048]{2,1,0:T(8,128)(2,1)S(1)}) custom-call(s32[3]{0:T(128)S(1)} %pad_add_fusion.at_ref, bf16[1,32,1,16,128]{4,3,2,1,0:T(8,128)(2,1)S(1)} %collective-permute-done.h_ref, bf16[288,512]{1,0:T(8,128)(2,1)S(1)} %get-tuple-element.33.zero_ref, ...), custom_call_target="tpu_custom_call" | custom-call | flops 10000000000 | bytes 8000000 | tf_op jit(solution)/shard_map/pallas_call | solution.py:318
  20.3 5.4 %collective-permute-start.1 = (bf16[4,8,2048]{2,1,0:T(8,128)(2,1)S(1)}, bf16[4,8,2048]{2,1,0:T(8,128)(2,1)S(1)}, u32[]{:S(2)}, u32[]{:S(2)}) collective-permute-start(bf16[4,8,2048]{2,1,0:T(8,128)(2,1)S(1)} %get-tuple-element.42), channel_id=1, source_target_pairs={{0,1},{1,0},{2,3},{3,2},{4,5},{5,4},{6,7},{7,6},{8,9},{9,8},{10,11... | collective-permute-start | bytes 393224 | tf_op jit(solution)/shard_map/ppermute | solution.py:326
  25.8 2.1 %all-to-all-done = bf16[8,8,2048]{2,1,0:T(8,128)(2,1)S(1)} async-done(((bf16[8,8,2048]{2,1,0:T(8,128)(2,1)}), bf16[8,8,2048]{2,1,0:T(8,128)(2,1)S(1)}, u32[]{:S(2)}, u32[]{:S(2)}) %all-to-all-start) | async-done | bytes 262176 | tf_op jit(solution)/shard_map/all_to_all | solution.py:290
  27.8 2.5 %shard_map.70 = (f32[768,128]{1,0:T(8,128)S(1)}, f32[768,128]{1,0:T(8,128)S(1)}) custom-call(s32[3]{0:T(128)S(1)} %pad_add_fusion.at_ref, bf16[288,512]{1,0:T(8,128)(2,1)S(1)} %get-tuple-element.37.u_ref, bf16[288,512]{1,0:T(8,128)(2,1)S(1)} %get-tuple-element.33.zero_ref, bf16[576,1024]{1,0:T(8,128)(2,1)S(1)} %get-tuple-element.34.rest_ref, ...), custom_call_target="tpu_custom_call" | custom-call | bytes 12000000 | tf_op jit(solution)/shard_map/pallas_call | solution.py:327
  30.4 1.3 %collective-permute-done.1.got_ref = bf16[4,8,2048]{2,1,0:T(8,128)(2,1)S(1)} collective-permute-done((bf16[4,8,2048]{2,1,0:T(8,128)(2,1)S(1)}, bf16[4,8,2048]{2,1,0:T(8,128)(2,1)S(1)}, u32[]{:S(2)}, u32[]{:S(2)}) %collective-permute-start.1) | collective-permute-done | bytes 131104 | tf_op jit(solution)/shard_map/ppermute | solution.py:326
  31.7 0.8 collective-permute-start.2
  32.5 0.6 shard_map.71
  33.1 0.8 collective-permute-done.2
  33.9 15.0 %all_to_all.20.x_ref = bf16[16,48,128]{2,1,0:T(8,128)(2,1)S(1)} all-to-all(bf16[16,48,128]{2,1,0:T(8,128)(2,1)S(1)} %bitcast.15), channel_id=1, replica_groups=mesh['zl'=4,'x'=4,'core'=2,'y'=4,'zh'=2] {'x','y'}, dimensions={0} | all-to-all | bytes 393216 | tf_op jit(solution)/shard_map/all_to_all | solution.py:290
  48.9 0.7 shard_map.72
  49.6 6.6 %all-to-all-start.2 = ((bf16[8,48,128]{2,1,0:T(8,128)(2,1)}), bf16[8,48,128]{2,1,0:T(8,128)(2,1)S(1)}, u32[]{:S(2)}, u32[]{:S(2)}) async-start(bf16[8,48,128]{2,1,0:T(8,128)(2,1)} %shard_map.72), calls=%async_computation.2 | async-start | bytes 196608 | tf_op jit(solution)/shard_map/all_to_all | solution.py:290
  56.2 0.1 collective-permute-start.3
  56.3 2.0 %collective-permute-start.4 = (bf16[8,3072]{1,0:T(8,128)(2,1)S(1)}, bf16[8,3072]{1,0:T(8,128)(2,1)S(1)}, u32[]{:S(2)}, u32[]{:S(2)}) collective-permute-start(bf16[8,3072]{1,0:T(8,128)(2,1)S(1)} %get-tuple-element.53), channel_id=1, source_target_pairs={{0,4},{2,6},{4,0},{6,2},{1,5},{3,7},{5,1},{7,3},{8,12},{10,14},{12... | collective-permute-start | bytes 147464 | tf_op jit(solution)/shard_map/ppermute | solution.py:349
  58.3 1.5 %collective-permute-start.5 = (bf16[8,3072]{1,0:T(8,128)(2,1)S(1)}, bf16[8,3072]{1,0:T(8,128)(2,1)S(1)}, u32[]{:S(2)}, u32[]{:S(2)}) collective-permute-start(bf16[8,3072]{1,0:T(8,128)(2,1)S(1)} %get-tuple-element.54), channel_id=1, source_target_pairs={{0,6},{2,0},{4,2},{6,4},{1,7},{3,1},{5,3},{7,5},{8,14},{10,8},{12,... | collective-permute-start | bytes 147464 | tf_op jit(solution)/shard_map/ppermute | solution.py:349
  59.7 3.2 %all-to-all-done.2.x_ref = bf16[8,48,128]{2,1,0:T(8,128)(2,1)S(1)} async-done(((bf16[8,48,128]{2,1,0:T(8,128)(2,1)}), bf16[8,48,128]{2,1,0:T(8,128)(2,1)S(1)}, u32[]{:S(2)}, u32[]{:S(2)}) %all-to-all-start.2) | async-done | bytes 98336 | tf_op jit(solution)/shard_map/all_to_all | solution.py:290
  62.9 0.0 collective-permute-done.3.one_ref
  63.0 0.0 collective-permute-done.4.two_ref
  63.0 0.0 collective-permute-done.5.three_ref
  63.0 10.2 %all_to_all.21 = bf16[16,48,128]{2,1,0:T(8,128)(2,1)S(1)} all-to-all(bf16[16,48,128]{2,1,0:T(8,128)(2,1)S(1)} %shard_map.73), channel_id=1, replica_groups=mesh['zl'=4,'x'=4,'core'=2,'y'=4,'zh'=2] {'x','y'}, dimensions={0} | all-to-all | bytes 393216 | tf_op jit(solution)/shard_map/all_to_all | solution.py:290
  73.2 4.4 %collective-permute-start.6 = (bf16[768,128]{1,0:T(8,128)(2,1)S(1)}, bf16[768,128]{1,0:T(8,128)(2,1)S(1)}, u32[]{:S(2)}, u32[]{:S(2)}) collective-permute-start(bf16[768,128]{1,0:T(8,128)(2,1)S(1)} %bitcast.13), channel_id=1, source_target_pairs={{0,8},{8,0},{1,9},{9,1},{2,10},{10,2},{3,11},{11,3},{4,12},{12,4},... | collective-permute-start | bytes 589832 | tf_op jit(solution)/shard_map/ppermute | solution.py:354
  77.6 1.6 %shard_map.74 = bf16[1,8,16,8,64]{4,3,2,1,0:T(8,128)(2,1)} custom-call(s32[3]{0:T(128)S(1)} %pad_add_fusion.at_ref, f32[8,3072]{1,0:T(8,128)S(1)} %get-tuple-element.50.own_ref, bf16[8,3072]{1,0:T(8,128)(2,1)S(1)} %collective-permute-done.3.one_ref, bf16[8,3072]{1,0:T(8,128)(2,1)S(1)} %collective-permute-done.4.two_ref, ...), custom_call_target="tpu_custom_call" | custom-call | bytes 10000 | tf_op jit(solution)/shard_map/pallas_call | solution.py:363
  79.3 0.0 collective-permute-done.6.other_ref
  79.3 1.8 %shard_map.75 = (f32[864,64]{1,0:T(8,128)}, f32[1728,64]{1,0:T(8,128)}) custom-call(s32[3]{0:T(128)S(1)} %pad_add_fusion.at_ref, bf16[768,128]{1,0:T(8,128)(2,1)S(1)} %bitcast.14, bf16[768,128]{1,0:T(8,128)(2,1)S(1)} %collective-permute-done.6.other_ref), custom_call_target="tpu_custom_call" | custom-call | flops 2000000000 | bytes 4000000 | tf_op jit(solution)/shard_map/pallas_call | solution.py:355
  (5 shorter events, 0.1 us)
Async XLA Ops:
  0.6 16.0 %copy-start = (bf16[1,32,4,16,128]{4,3,2,1,0:T(8,128)(2,1)S(1)}, bf16[1,32,4,16,128]{4,3,2,1,0:T(8,128)(2,1)}, u32[]{:S(2)}) copy-start(bf16[1,32,4,16,128]{4,3,2,1,0:T(8,128)(2,1)} %v_ref.3) | copy-start | bytes 1572868
  0.6 16.0 %copy-start.1 = (bf16[27,64,64]{2,1,0:T(8,128)(2,1)S(1)}, bf16[27,64,64]{2,1,0:T(8,128)(2,1)}, u32[]{:S(2)}) copy-start(bf16[27,64,64]{2,1,0:T(8,128)(2,1)} %param.6) | copy-start | bytes 663556
  0.7 16.0 %copy-start.2 = (bf16[27,32,64]{2,1,0:T(8,128)(2,1)S(1)}, bf16[27,32,64]{2,1,0:T(8,128)(2,1)}, u32[]{:S(2)}) copy-start(bf16[27,32,64]{2,1,0:T(8,128)(2,1)} %param.5) | copy-start | bytes 331780
  2.8 15.3 %collective-permute-start = (bf16[1,32,1,16,128]{4,3,2,1,0:T(8,128)(2,1)}, bf16[1,32,1,16,128]{4,3,2,1,0:T(8,128)(2,1)S(1)}, u32[]{:S(2)}, u32[]{:S(2)}) collective-permute-start(bf16[1,32,1,16,128]{4,3,2,1,0:T(8,128)(2,1)} %get-tuple-element.32), channel_id=1, source_target_pairs={{0,1},{1,2},{2,3},{3,4},{4,5},{5,6},{6,7},{8,9},{9,10},{10,11},{11... | collective-permute-start | bytes 393224 | tf_op jit(solution)/shard_map/ppermute | solution.py:286
  12.4 15.4 %all-to-all-start = ((bf16[8,8,2048]{2,1,0:T(8,128)(2,1)}), bf16[8,8,2048]{2,1,0:T(8,128)(2,1)S(1)}, u32[]{:S(2)}, u32[]{:S(2)}) async-start(bf16[8,8,2048]{2,1,0:T(8,128)(2,1)} %get-tuple-element.39), calls=%async_computation | async-start | bytes 524288 | tf_op jit(solution)/shard_map/all_to_all | solution.py:290
  20.3 11.4 %collective-permute-start.1 = (bf16[4,8,2048]{2,1,0:T(8,128)(2,1)S(1)}, bf16[4,8,2048]{2,1,0:T(8,128)(2,1)S(1)}, u32[]{:S(2)}, u32[]{:S(2)}) collective-permute-start(bf16[4,8,2048]{2,1,0:T(8,128)(2,1)S(1)} %get-tuple-element.42), channel_id=1, source_target_pairs={{0,1},{1,0},{2,3},{3,2},{4,5},{5,4},{6,7},{7,6},{8,9},{9,8},{10,11... | collective-permute-start | bytes 393224 | tf_op jit(solution)/shard_map/ppermute | solution.py:326
  31.7 2.1 %collective-permute-start.2 = (f32[768,128]{1,0:T(8,128)S(1)}, f32[768,128]{1,0:T(8,128)S(1)}, u32[]{:S(2)}, u32[]{:S(2)}) collective-permute-start(f32[768,128]{1,0:T(8,128)S(1)} %get-tuple-element.43), channel_id=1, source_target_pairs={{0,8},{8,0},{1,9},{9,1},{2,10},{10,2},{3,11},{11,3},{4,12},{12,4},... | collective-permute-start | bytes 1179656 | tf_op jit(solution)/shard_map/ppermute | solution.py:340
  49.6 13.3 %all-to-all-start.2 = ((bf16[8,48,128]{2,1,0:T(8,128)(2,1)}), bf16[8,48,128]{2,1,0:T(8,128)(2,1)S(1)}, u32[]{:S(2)}, u32[]{:S(2)}) async-start(bf16[8,48,128]{2,1,0:T(8,128)(2,1)} %shard_map.72), calls=%async_computation.2 | async-start | bytes 196608 | tf_op jit(solution)/shard_map/all_to_all | solution.py:290
  56.2 6.8 %collective-permute-start.3 = (bf16[8,3072]{1,0:T(8,128)(2,1)S(1)}, bf16[8,3072]{1,0:T(8,128)(2,1)S(1)}, u32[]{:S(2)}, u32[]{:S(2)}) collective-permute-start(bf16[8,3072]{1,0:T(8,128)(2,1)S(1)} %get-tuple-element.52), channel_id=1, source_target_pairs={{0,2},{2,4},{4,6},{6,0},{1,3},{3,5},{5,7},{7,1},{8,10},{10,12},{12... | collective-permute-start | bytes 147464 | tf_op jit(solution)/shard_map/ppermute | solution.py:349
  56.3 6.7 %collective-permute-start.4 = (bf16[8,3072]{1,0:T(8,128)(2,1)S(1)}, bf16[8,3072]{1,0:T(8,128)(2,1)S(1)}, u32[]{:S(2)}, u32[]{:S(2)}) collective-permute-start(bf16[8,3072]{1,0:T(8,128)(2,1)S(1)} %get-tuple-element.53), channel_id=1, source_target_pairs={{0,4},{2,6},{4,0},{6,2},{1,5},{3,7},{5,1},{7,3},{8,12},{10,14},{12... | collective-permute-start | bytes 147464 | tf_op jit(solution)/shard_map/ppermute | solution.py:349
  58.3 4.7 %collective-permute-start.5 = (bf16[8,3072]{1,0:T(8,128)(2,1)S(1)}, bf16[8,3072]{1,0:T(8,128)(2,1)S(1)}, u32[]{:S(2)}, u32[]{:S(2)}) collective-permute-start(bf16[8,3072]{1,0:T(8,128)(2,1)S(1)} %get-tuple-element.54), channel_id=1, source_target_pairs={{0,6},{2,0},{4,2},{6,4},{1,7},{3,1},{5,3},{7,5},{8,14},{10,8},{12,... | collective-permute-start | bytes 147464 | tf_op jit(solution)/shard_map/ppermute | solution.py:349
  73.2 6.1 %collective-permute-start.6 = (bf16[768,128]{1,0:T(8,128)(2,1)S(1)}, bf16[768,128]{1,0:T(8,128)(2,1)S(1)}, u32[]{:S(2)}, u32[]{:S(2)}) collective-permute-start(bf16[768,128]{1,0:T(8,128)(2,1)S(1)} %bitcast.13), channel_id=1, source_target_pairs={{0,8},{8,0},{1,9},{9,1},{2,10},{10,2},{3,11},{11,3},{4,12},{12,4},... | collective-permute-start | bytes 589832 | tf_op jit(solution)/shard_map/ppermute | solution.py:354

commit v3 on v2

--- a/solution.py
+++ b/solution.py
@@ -146,7 +146,7 @@
     two_ref[...] = jnp.concatenate([k_ref[a * 576 : (a + 1) * 576, :] for a in range(3)], axis=1)
 
 
-def first_block(at_ref, h_ref, zero_ref, rest_ref, one_ref, two_ref, u_ref, act_ref, keep_ref, send_ref, halo, spots, parts):
+def first_block(h_ref, zero_ref, rest_ref, one_ref, two_ref, u_ref, act_ref, up_0, up_1, up_2, up_3, halo, spots, parts):
     halo[...] = jnp.dot(h_ref[0].reshape(512, 128), column_split(), preferred_element_type=F)
     row, col = cell_index((C0, CELLS))
     for at, value in deinterleave(lambda line: halo[pl.ds(line, C0, stride=16), :], row, col):
@@ -164,15 +164,12 @@
     slots = (early[ahead], early[same] + late[ahead], early[back] + late[same], late[back])
     for slot, value in enumerate(slots):
         parts[:, slot * CELLS : (slot + 1) * CELLS] = value
-    side = at_ref[1]
-    for group in range(4):
-        own = pl.multiple_of(group * 16 + side * 8, 8)
-        other = pl.multiple_of(group * 16 + (1 - side) * 8, 8)
-        keep_ref[group] = parts[pl.ds(own, 8), :]
-        send_ref[group] = parts[pl.ds(other, 8), :].astype(BF)
-
-
-def gradients(at_ref, u_ref, zero_ref, rest_ref, act_ref, g_ref, two_ref, mine_ref, other_ref, depths, spots, both):
+    for step, ref in enumerate((up_0, up_1, up_2, up_3)):
+        rows = pl.multiple_of(lax.rem(lax.axis_index("y") + step, 4) * 16, 16)
+        ref[...] = parts[pl.ds(rows, 16), :].astype(ref.dtype)
+
+
+def gradients(u_ref, zero_ref, rest_ref, act_ref, g_ref, two_ref, mine_ref, other_ref, depths, spots, both):
     for a in range(3):
         depths[a * C1 : (a + 1) * C1, :] = g_ref[:, (2 - a) * CELLS : (2 - a) * CELLS + SLAB]
     shape = (C1, SLAB)
@@ -202,31 +199,34 @@
     both[864:1008, :] = jnp.concatenate([first[0:144, :], first[144:288, :]], axis=1)
     both[1008:1296, :] = jnp.concatenate([rest[0:288, :], rest[288:576, :]], axis=1)
     both[1296:ROWS, :] = jnp.zeros((ROWS - 1296, 128), F)
-    core = at_ref[0]
+    core = lax.axis_index("core")
     mine_ref[...] = both[pl.ds(pl.multiple_of(core * HALF, HALF), HALF), :]
     other_ref[...] = both[pl.ds(pl.multiple_of((1 - core) * HALF, HALF), HALF), :]
 
 
-def join_sides(at_ref, keep_ref, got_ref, *o_refs):
-    lower = at_ref[1] == 0
-    for step, o_ref in enumerate(o_refs):
-        group = lax.rem(at_ref[2] + step, 4)
-        kept, got = keep_ref[group], got_ref[group].astype(F)
-        first, second = jnp.where(lower, kept, got), jnp.where(lower, got, kept)
-        middle = first[:, 2 * CELLS :] + second[:, : 2 * CELLS]
-        joined = jnp.concatenate([first[:, : 2 * CELLS], middle, second[:, 2 * CELLS :]], axis=1)
-        o_ref[...] = joined.astype(o_ref.dtype)
-
-
-def unpack_features(at_ref, own_ref, one_ref, two_ref, three_ref, o_ref, groups, flat):
+def split_sides(own_ref, one_ref, two_ref, three_ref, keep_ref, send_ref):
+    lower = lax.axis_index("zh") == 0
     for step, ref in enumerate((own_ref, one_ref, two_ref, three_ref)):
-        groups[lax.rem(at_ref[2] + 4 - step, 4)] = ref[...].astype(F)
+        source = lax.rem(lax.axis_index("y") + 4 - step, 4)
+        value = ref[...].astype(F)
+        first, second = value[0:8], value[8:16]
+        keep_ref[source] = jnp.where(lower, first, second)
+        send_ref[source, :, 0 : 4 * CELLS] = jnp.where(lower, second, first).astype(BF)
+        send_ref[source, :, 4 * CELLS :] = jnp.zeros((8, 2 * CELLS), BF)
+
+
+def unpack_features(keep_ref, got_ref, o_ref, slabs, flat):
+    side = lax.axis_index("zh")
+    for group in range(4):
+        slabs[2 * group + side] = keep_ref[group]
+        slabs[2 * group + 1 - side] = got_ref[group, :, 0 : 4 * CELLS].astype(F)
     for plane in range(16):
-        group, at = plane // 4, plane % 4 + 1
-        value = groups[group, :, at * CELLS : (at + 1) * CELLS]
-        near, slot = {1: (group - 1, 5), 4: (group + 1, 0)}.get(at, (-1, 0))
-        if 0 <= near < 4:
-            value = value + groups[near, :, slot * CELLS : (slot + 1) * CELLS]
+        slab, depth = plane // 2, plane % 2
+        at = (1 + depth) * CELLS
+        value = slabs[slab, :, at : at + CELLS]
+        near, slot = (slab - 1, 3) if depth == 0 else (slab + 1, 0)
+        if 0 <= near < 8:
+            value = value + slabs[near, :, slot * CELLS : (slot + 1) * CELLS]
         for pair in range(4):
             tile = value[:, pair * 128 : (pair + 1) * 128]
             line = plane * 8 + 2 * pair
@@ -244,8 +244,8 @@
         o_ref[at] = total
 
 
-def unpack_gradients(at_ref, mine_ref, other_ref, one_ref, two_ref, both):
-    core = at_ref[0]
+def unpack_gradients(mine_ref, other_ref, one_ref, two_ref, both):
+    core = lax.axis_index("core")
     both[pl.ds(pl.multiple_of(core * HALF, HALF), HALF), :] = mine_ref[...].astype(F)
     both[pl.ds(pl.multiple_of((1 - core) * HALF, HALF), HALF), :] = other_ref[...].astype(F)
     two_ref[0:576, :] = both[0:576, 0:64]
@@ -262,19 +262,6 @@
     return jax.ShapeDtypeStruct(shape, dtype)
 
 
-def with_place(kernel, outs, operands, scratch, flops, moved):
-    whole = pl.BlockSpec(memory_space=pltpu.VMEM)
-    return pl.pallas_call(
-        kernel,
-        in_specs=[pl.BlockSpec(memory_space=pltpu.SMEM)] + [whole] * operands,
-        out_specs=[whole] * len(outs),
-        out_shape=outs,
-        scratch_shapes=scratch,
-        compiler_params=pltpu.CompilerParams(vmem_limit_bytes=LIMIT),
-        cost_estimate=pl.CostEstimate(flops=flops, bytes_accessed=moved, transcendentals=0),
-    )
-
-
 SPACE = ("y", "zh")
 PLANE = ("x", "y")
 LINE = ("zl", "zh")
@@ -291,7 +278,6 @@
 
 
 def shards(volumes, w_first, w_second, grad_out):
-    place = jnp.stack([lax.axis_index("core"), lax.axis_index("zh"), lax.axis_index("y")]).astype(jnp.int32)
     kernel_one = w_first.reshape(27 * C0, C1)
     kernel_two = w_second.reshape(27 * C1, C1)
     far = pl.BlockSpec(memory_space=pltpu.HBM)
@@ -315,59 +301,57 @@
         0,
         COST_OWN,
     )(volumes, kernel_one, kernel_two)
-    taps, act, keep, send = with_place(
+    chunk = (16, 4 * CELLS)
+    taps, act, *sent = call(
         first_block,
-        [sds((9 * C0, CELLS), BF), sds((C1, SLAB), BF), sds((4, 8, 4 * CELLS), F), sds((4, 8, 4 * CELLS), BF)],
-        5,
+        [sds((9 * C0, CELLS), BF), sds((C1, SLAB), BF), sds(chunk, F)] + [sds(chunk, BF)] * 3,
         [pltpu.VMEM((512, 128), F), pltpu.VMEM((9 * C1, SLAB), BF), pltpu.VMEM((C1, 4 * CELLS), F)],
         FLOPS_FIRST,
         COST_FIRST,
-    )(place, lower, zero, rest, one, two)
-    got = lax.ppermute(send, "zh", [(0, 1), (1, 0)])
-    mine, other = with_place(
+    )(lower, zero, rest, one, two)
+    arrived = [
+        lax.ppermute(sent[step], "y", [(at, (at + step) % 4) for at in range(4)]) for step in range(1, 4)
+    ]
+    mine, other = call(
         gradients,
         [sds((HALF, 128), F), sds((HALF, 128), F)],
-        6,
         [pltpu.VMEM((3 * C1, SLAB), BF), pltpu.VMEM((9 * C1, SLAB), BF), pltpu.VMEM((ROWS, 128), F)],
         FLOPS_GRAD,
         COST_GRAD,
-    )(place, taps, zero, rest, act, cotangent, two)
+    )(taps, zero, rest, act, cotangent, two)
     cores = lax.axis_size("core")
     pairs = [(at, at ^ 1) for at in range(cores)]
-    other, got = lax.optimization_barrier((other, got))
-    side = (8, 6 * CELLS)
-    joined = with_place(join_sides, [sds(side, F)] + [sds(side, BF)] * 3, 2, [], 0, 10000)(place, keep, got)
+    other, arrived = lax.optimization_barrier((other, arrived))
+    keep, send = call(split_sides, [sds((4, 8, 4 * CELLS), F), sds((4, 8, 6 * CELLS), BF)], [], 0, 10000)(
+        sent[0], *arrived
+    )
     chip = mine + lax.ppermute(other, "core", pairs)
-    chip, joined = lax.optimization_barrier((chip.astype(SENT), joined))
+    chip, send = lax.optimization_barrier((chip.astype(SENT), send))
     count = lax.axis_size("x") * lax.axis_size("y")
     deep = lax.axis_size("zl") * lax.axis_size("zh")
     share = HALF // count
     plane_parts = exchange(chip.reshape(count, share, 128), PLANE)
     line_in = call(sum_and_spread, sds((deep, share, 128), SENT), (), 0, 10000)(plane_parts)
     line_parts = exchange(line_in, LINE)
-    moved = [
-        lax.ppermute(joined[step], "y", [(at, (at + step) % 4) for at in range(4)]) for step in range(1, 4)
-    ]
+    got = lax.ppermute(send, "zh", [(0, 1), (1, 0)])
     plane_in = call(sum_and_spread, sds((count, share, 128), SENT), (), 0, 10000)(line_parts)
-    plane_in, moved = lax.optimization_barrier((plane_in, moved))
+    plane_in, got = lax.optimization_barrier((plane_in, got))
     my_half = exchange(plane_in, PLANE).reshape(HALF, 128)
     other_half = lax.ppermute(my_half, "core", pairs)
-    total_one, total_two = with_place(
+    total_one, total_two = call(
         unpack_gradients,
         [sds((27 * C0, C1), F), sds((27 * C1, C1), F)],
-        2,
         [pltpu.VMEM((ROWS, 128), F)],
         FLOPS_LAST,
         4000000,
-    )(place, my_half, other_half)
-    features = with_place(
+    )(my_half, other_half)
+    features = call(
         unpack_features,
         [sds((1, 8, 16, 8, 64), BF)],
-        4,
-        [pltpu.VMEM((4,) + side, F), pltpu.VMEM((1024, 128), F)],
+        [pltpu.VMEM((8, 8, 4 * CELLS), F), pltpu.VMEM((1024, 128), F)],
         0,
         10000,
-    )(place, joined[0], *moved)[0]
+    )(keep, got)[0]
     return features, total_one.reshape(27, C0, C1), total_two.reshape(27, C1, C1)
 
 

time: 81.5 us -> 78.5 us (0.963)
  Pallas kernels: 13 us -> 9.72 us
  blocking collectives: 25.2 us -> 27.3 us
  waiting for transfers between devices: 7.38 us -> 5.86 us
  starting transfers between devices: 34.6 us -> 33.7 us
    pallas_call x5, Pallas kernels: 8.84 us -> 6.24 us  [the longest x1 2 us: shards(): call(gradients, [sds((HALF, 128), F), sds((HALF, 128), F)], [pltpu.VMEM((...]
    all_to_all x2, blocking collectives: 25.2 us -> 27.3 us  [exchange(): return lax.all_to_all(value, axes, split_axis=0, concat_axis=0, tiled=True)]
    ppermute x1, starting transfers between devices: 4.41 us -> 2.41 us  [shards(): other_half = lax.ppermute(my_half, 'core', pairs)]
    all_to_all x2, starting transfers between devices: 10.8 us -> 9.03 us  [exchange(): return lax.all_to_all(value, axes, split_axis=0, concat_axis=0, tiled=True)]
    ppermute x3, starting transfers between devices: 3.55 us -> 5.11 us  [shards(): lax.ppermute(sent[step], 'y', [(at, (at + step) % 4) for at in range(4)])]
    ppermute x1, waiting for transfers between devices: 1.35 us -> 0.01 us  [shards(): got = lax.ppermute(send, 'zh', [(0, 1), (1, 0)])]
    ppermute x1, starting transfers between devices: 0.77 us -> 1.99 us  [shards(): chip = mine + lax.ppermute(other, 'core', pairs)]
  transfers between devices with their start and end apart: 9 -> 9, of which waited for: 4 -> 3; matrix products, arithmetic and copies ran while one was open for 0% -> 0% of each run, Pallas kernels for 10% -> 8%
where the time goes in v3:
time: 78.5 us; the launch traced here: 78.1 us
  starting transfers between devices  33.7 us (43%)
  blocking collectives  27.3 us (35%)
  Pallas kernels  9.72 us (12%)
  waiting for transfers between devices  5.86 us (7%)
    all_to_all x2, blocking collectives, exchange(): return lax.all_to_all(value, axes, split_axis=0, concat_axis=0, tiled=True)  27.3 us
    ppermute x1, starting transfers between devices, along(): return lax.ppermute(value, SPACE, pairs)  9.65 us
    all_to_all x2, starting transfers between devices, exchange(): return lax.all_to_all(value, axes, split_axis=0, concat_axis=0, tiled=True)  9.03 us
    ppermute x1, starting transfers between devices, shards(): got = lax.ppermute(send, 'zh', [(0, 1), (1, 0)])  5.5 us
    ppermute x3, starting transfers between devices, shards(): lax.ppermute(sent[step], 'y', [(at, (at + step) % 4) for at in range(4)])  5.11 us
    all_to_all x2, waiting for transfers between devices, exchange(): return lax.all_to_all(value, axes, split_axis=0, concat_axis=0, tiled=True)  4.55 us
    ppermute x1, starting transfers between devices, shards(): other_half = lax.ppermute(my_half, 'core', pairs)  2.41 us
    pallas_call x1, Pallas kernels, shards(): call(pack_inputs, [sds((8, 8, 2048), BF), sds((1, C0, 1, 16, 128), BF)],...  2.12 us
  transfers between devices with their start and end apart: 9, of which 3 were waited for; matrix products, arithmetic and copies ran while one was open for 0% of the time, Pallas kernels for 8%

profile of v3, /device:TPU:1, one launch (start us, length us, event | category | flops | bytes accessed | tf_op | source)
XLA Modules:
  0.0 78.1 jit_solution(2151900759387179082)
XLA Ops:
  0.6 0.0 copy-start
  0.6 0.0 copy-start.1
  0.7 0.0 copy-start.2
  0.7 2.1 %shard_map.67 = (bf16[8,8,2048]{2,1,0:T(8,128)(2,1)}, bf16[1,32,1,16,128]{4,3,2,1,0:T(8,128)(2,1)}) custom-call(bf16[1,8,16,8,64]{4,3,2,1,0:T(8,128)(2,1)} %x_ref.1, bf16[1,32,4,16,128]{4,3,2,1,0:T(8,128)(2,1)} %v_ref.3), custom_call_target="tpu_custom_call" | custom-call | bytes 4000000 | tf_op jit(solution)/shard_map/pallas_call | solution.py:285
  2.8 9.6 %collective-permute-start = (bf16[1,32,1,16,128]{4,3,2,1,0:T(8,128)(2,1)}, bf16[1,32,1,16,128]{4,3,2,1,0:T(8,128)(2,1)S(1)}, u32[]{:S(2)}, u32[]{:S(2)}) collective-permute-start(bf16[1,32,1,16,128]{4,3,2,1,0:T(8,128)(2,1)} %get-tuple-element.29), channel_id=1, source_target_pairs={{0,1},{1,2},{2,3},{3,4},{4,5},{5,6},{6,7},{8,9},{9,10},{10,11},{11... | collective-permute-start | bytes 393224 | tf_op jit(solution)/shard_map/ppermute | solution.py:273
  12.4 4.2 %all-to-all-start = ((bf16[8,8,2048]{2,1,0:T(8,128)(2,1)}), bf16[8,8,2048]{2,1,0:T(8,128)(2,1)S(1)}, u32[]{:S(2)}, u32[]{:S(2)}) async-start(bf16[8,8,2048]{2,1,0:T(8,128)(2,1)} %get-tuple-element.37), calls=%async_computation | async-start | bytes 524288 | tf_op jit(solution)/shard_map/all_to_all | solution.py:277
  16.6 0.0 copy-done
  16.7 1.3 %shard_map.68 = (bf16[288,512]{1,0:T(8,128)(2,1)S(1)}, bf16[576,1024]{1,0:T(8,128)(2,1)S(1)}, bf16[864,64]{1,0:T(8,128)(2,1)S(1)}, bf16[576,192]{1,0:T(8,128)(2,1)S(1)}) custom-call(bf16[1,32,4,16,128]{4,3,2,1,0:T(8,128)(2,1)S(1)} %copy-done, bf16[864,64]{1,0:T(8,128)(2,1)S(1)} %bitcast.9, bf16[1728,64]{1,0:T(8,128)(2,1)S(1)} %bitcast.8), custom_call_target="tpu_custom_call" | custom-call | bytes 12000000 | tf_op jit(solution)/shard_map/pallas_call | solution.py:297
  18.0 0.0 collective-permute-done.h_ref
  18.0 1.7 %shard_map.69 = (bf16[288,512]{1,0:T(8,128)(2,1)S(1)}, bf16[64,1024]{1,0:T(8,128)(2,1)S(1)}, f32[16,2048]{1,0:T(8,128)S(1)}, bf16[16,2048]{1,0:T(8,128)(2,1)S(1)...) custom-call(bf16[1,32,1,16,128]{4,3,2,1,0:T(8,128)(2,1)S(1)} %collective-permute-done.h_ref, ...), custom_call_target="tpu_custom_call" | custom-call | flops 10000000000 | bytes 8000000 | tf_op jit(solution)/shard_map/pallas_call | solution.py:305
  19.7 1.5 %collective-permute-start.1 = (bf16[16,2048]{1,0:T(8,128)(2,1)S(1)}, bf16[16,2048]{1,0:T(8,128)(2,1)S(1)}, u32[]{:S(2)}, u32[]{:S(2)}) collective-permute-start(bf16[16,2048]{1,0:T(8,128)(2,1)S(1)} %get-tuple-element.39), channel_id=1, source_target_pairs={{0,2},{2,4},{4,6},{6,0},{1,3},{3,5},{5,7},{7,1},{8,10},{10,12},{12... | collective-permute-start | bytes 196616 | tf_op jit(solution)/shard_map/ppermute | solution.py:313
  21.3 2.4 %collective-permute-start.2 = (bf16[16,2048]{1,0:T(8,128)(2,1)S(1)}, bf16[16,2048]{1,0:T(8,128)(2,1)S(1)}, u32[]{:S(2)}, u32[]{:S(2)}) collective-permute-start(bf16[16,2048]{1,0:T(8,128)(2,1)S(1)} %get-tuple-element.40), channel_id=1, source_target_pairs={{0,4},{2,6},{4,0},{6,2},{1,5},{3,7},{5,1},{7,3},{8,12},{10,14},{12... | collective-permute-start | bytes 196616 | tf_op jit(solution)/shard_map/ppermute | solution.py:313
  23.7 1.2 %collective-permute-start.3 = (bf16[16,2048]{1,0:T(8,128)(2,1)S(1)}, bf16[16,2048]{1,0:T(8,128)(2,1)S(1)}, u32[]{:S(2)}, u32[]{:S(2)}) collective-permute-start(bf16[16,2048]{1,0:T(8,128)(2,1)S(1)} %get-tuple-element.41), channel_id=1, source_target_pairs={{0,6},{2,0},{4,2},{6,4},{1,7},{3,1},{5,3},{7,5},{8,14},{10,8},{12,... | collective-permute-start | bytes 196616 | tf_op jit(solution)/shard_map/ppermute | solution.py:313
  24.8 3.0 %all-to-all-done = bf16[8,8,2048]{2,1,0:T(8,128)(2,1)S(1)} async-done(((bf16[8,8,2048]{2,1,0:T(8,128)(2,1)}), bf16[8,8,2048]{2,1,0:T(8,128)(2,1)S(1)}, u32[]{:S(2)}, u32[]{:S(2)}) %all-to-all-start) | async-done | bytes 262176 | tf_op jit(solution)/shard_map/all_to_all | solution.py:277
  27.8 2.0 %shard_map.70 = (f32[768,128]{1,0:T(8,128)S(1)}, f32[768,128]{1,0:T(8,128)S(1)}) custom-call(bf16[288,512]{1,0:T(8,128)(2,1)S(1)} %get-tuple-element.35.u_ref, bf16[288,512]{1,0:T(8,128)(2,1)S(1)} %get-tuple-element.30.zero_ref, bf16[576,1024]{1,0:T(8,128)(2,1)S(1)} %get-tuple-element.31.rest_ref, bf16[64,1024]{1,0:T(8,128)(2,1)S(1)} %get-tuple-element.36.act_ref, ...), custom_call_target="tpu_custom_call" | custom-call | bytes 12000000 | tf_op jit(solution)/shard_map/pallas_call | solution.py:315
  29.8 0.0 collective-permute-done.1.one_ref
  29.8 0.0 collective-permute-done.2.two_ref
  29.9 0.0 collective-permute-done.3.three_ref
  29.9 2.0 %collective-permute-start.4 = (f32[768,128]{1,0:T(8,128)S(1)}, f32[768,128]{1,0:T(8,128)S(1)}, u32[]{:S(2)}, u32[]{:S(2)}) collective-permute-start(f32[768,128]{1,0:T(8,128)S(1)} %get-tuple-element.47), channel_id=1, source_target_pairs={{0,8},{8,0},{1,9},{9,1},{2,10},{10,2},{3,11},{11,3},{4,12},{12,4},... | collective-permute-start | bytes 1179656 | tf_op jit(solution)/shard_map/ppermute | solution.py:328
  31.9 0.1 shard_map.71
  31.9 1.3 %collective-permute-done.4 = f32[768,128]{1,0:T(8,128)S(1)} collective-permute-done((f32[768,128]{1,0:T(8,128)S(1)}, f32[768,128]{1,0:T(8,128)S(1)}, u32[]{:S(2)}, u32[]{:S(2)}) %collective-permute-start.4) | collective-permute-done | bytes 393248 | tf_op jit(solution)/shard_map/ppermute | solution.py:328
  33.2 0.7 add_convert_fusion
  33.9 4.8 %all-to-all-start.1 = ((bf16[16,48,128]{2,1,0:T(8,128)(2,1)}), bf16[16,48,128]{2,1,0:T(8,128)(2,1)S(1)}, u32[]{:S(2)}, u32[]{:S(2)}) async-start(bf16[16,48,128]{2,1,0:T(8,128)(2,1)} %bitcast.3), calls=%async_computation.1 | async-start | bytes 393216 | tf_op jit(solution)/shard_map/all_to_all | solution.py:277
  38.8 5.5 %collective-permute-start.5 = (bf16[4,8,3072]{2,1,0:T(8,128)(2,1)S(1)}, bf16[4,8,3072]{2,1,0:T(8,128)(2,1)S(1)}, u32[]{:S(2)}, u32[]{:S(2)}) collective-permute-start(bf16[4,8,3072]{2,1,0:T(8,128)(2,1)S(1)} %get-tuple-element.50), channel_id=1, source_target_pairs={{0,1},{1,0},{2,3},{3,2},{4,5},{5,4},{6,7},{7,6},{8,9},{9,8},{10,11... | collective-permute-start | bytes 589832 | tf_op jit(solution)/shard_map/ppermute | solution.py:336
  44.3 1.6 %all-to-all-done.1.x_ref = bf16[16,48,128]{2,1,0:T(8,128)(2,1)S(1)} async-done(((bf16[16,48,128]{2,1,0:T(8,128)(2,1)}), bf16[16,48,128]{2,1,0:T(8,128)(2,1)S(1)}, u32[]{:S(2)}, u32[]{:S(2)}) %all-to-all-start.1) | async-done | bytes 196640 | tf_op jit(solution)/shard_map/all_to_all | solution.py:277
  45.9 14.6 %all_to_all.20.x_ref = bf16[8,48,128]{2,1,0:T(8,128)(2,1)S(1)} all-to-all(bf16[8,48,128]{2,1,0:T(8,128)(2,1)S(1)} %shard_map.72), channel_id=1, replica_groups=mesh['zl'=4,'x'=4,'core'=2,'y'=4,'zh'=2] {'zl','zh'}, dimensions={0} | all-to-all | bytes 196608 | tf_op jit(solution)/shard_map/all_to_all | solution.py:277
  60.5 0.0 collective-permute-done.5.got_ref
  60.5 12.7 %all_to_all.21 = bf16[16,48,128]{2,1,0:T(8,128)(2,1)S(1)} all-to-all(bf16[16,48,128]{2,1,0:T(8,128)(2,1)S(1)} %shard_map.73), channel_id=1, replica_groups=mesh['zl'=4,'x'=4,'core'=2,'y'=4,'zh'=2] {'x','y'}, dimensions={0} | all-to-all | bytes 393216 | tf_op jit(solution)/shard_map/all_to_all | solution.py:277
  73.2 2.4 %collective-permute-start.6 = (bf16[768,128]{1,0:T(8,128)(2,1)S(1)}, bf16[768,128]{1,0:T(8,128)(2,1)S(1)}, u32[]{:S(2)}, u32[]{:S(2)}) collective-permute-start(bf16[768,128]{1,0:T(8,128)(2,1)S(1)} %bitcast.10), channel_id=1, source_target_pairs={{0,8},{8,0},{1,9},{9,1},{2,10},{10,2},{3,11},{11,3},{4,12},{12,4},... | collective-permute-start | bytes 589832 | tf_op jit(solution)/shard_map/ppermute | solution.py:340
  75.6 1.1 %shard_map.74 = bf16[1,8,16,8,64]{4,3,2,1,0:T(8,128)(2,1)} custom-call(f32[4,8,2048]{2,1,0:T(8,128)S(1)} %get-tuple-element.45.keep_ref, bf16[4,8,3072]{2,1,0:T(8,128)(2,1)S(1)} %collective-permute-done.5.got_ref), custom_call_target="tpu_custom_call" | custom-call | bytes 10000 | tf_op jit(solution)/shard_map/pallas_call | solution.py:348
  76.8 0.0 collective-permute-done.6.other_ref
  76.8 1.3 %shard_map.75 = (f32[864,64]{1,0:T(8,128)}, f32[1728,64]{1,0:T(8,128)}) custom-call(bf16[768,128]{1,0:T(8,128)(2,1)S(1)} %bitcast.11, bf16[768,128]{1,0:T(8,128)(2,1)S(1)} %collective-permute-done.6.other_ref), custom_call_target="tpu_custom_call" | custom-call | flops 2000000000 | bytes 4000000 | tf_op jit(solution)/shard_map/pallas_call | solution.py:341
  (4 shorter events, 0.1 us)
Async XLA Ops:
  0.6 16.0 %copy-start = (bf16[1,32,4,16,128]{4,3,2,1,0:T(8,128)(2,1)S(1)}, bf16[1,32,4,16,128]{4,3,2,1,0:T(8,128)(2,1)}, u32[]{:S(2)}) copy-start(bf16[1,32,4,16,128]{4,3,2,1,0:T(8,128)(2,1)} %v_ref.3) | copy-start | bytes 1572868
  0.6 16.0 %copy-start.1 = (bf16[27,64,64]{2,1,0:T(8,128)(2,1)S(1)}, bf16[27,64,64]{2,1,0:T(8,128)(2,1)}, u32[]{:S(2)}) copy-start(bf16[27,64,64]{2,1,0:T(8,128)(2,1)} %param.6) | copy-start | bytes 663556
  0.7 16.0 %copy-start.2 = (bf16[27,32,64]{2,1,0:T(8,128)(2,1)S(1)}, bf16[27,32,64]{2,1,0:T(8,128)(2,1)}, u32[]{:S(2)}) copy-start(bf16[27,32,64]{2,1,0:T(8,128)(2,1)} %param.5) | copy-start | bytes 331780
  2.8 15.2 %collective-permute-start = (bf16[1,32,1,16,128]{4,3,2,1,0:T(8,128)(2,1)}, bf16[1,32,1,16,128]{4,3,2,1,0:T(8,128)(2,1)S(1)}, u32[]{:S(2)}, u32[]{:S(2)}) collective-permute-start(bf16[1,32,1,16,128]{4,3,2,1,0:T(8,128)(2,1)} %get-tuple-element.29), channel_id=1, source_target_pairs={{0,1},{1,2},{2,3},{3,4},{4,5},{5,6},{6,7},{8,9},{9,10},{10,11},{11... | collective-permute-start | bytes 393224 | tf_op jit(solution)/shard_map/ppermute | solution.py:273
  12.4 15.4 %all-to-all-start = ((bf16[8,8,2048]{2,1,0:T(8,128)(2,1)}), bf16[8,8,2048]{2,1,0:T(8,128)(2,1)S(1)}, u32[]{:S(2)}, u32[]{:S(2)}) async-start(bf16[8,8,2048]{2,1,0:T(8,128)(2,1)} %get-tuple-element.37), calls=%async_computation | async-start | bytes 524288 | tf_op jit(solution)/shard_map/all_to_all | solution.py:277
  19.7 10.1 %collective-permute-start.1 = (bf16[16,2048]{1,0:T(8,128)(2,1)S(1)}, bf16[16,2048]{1,0:T(8,128)(2,1)S(1)}, u32[]{:S(2)}, u32[]{:S(2)}) collective-permute-start(bf16[16,2048]{1,0:T(8,128)(2,1)S(1)} %get-tuple-element.39), channel_id=1, source_target_pairs={{0,2},{2,4},{4,6},{6,0},{1,3},{3,5},{5,7},{7,1},{8,10},{10,12},{12... | collective-permute-start | bytes 196616 | tf_op jit(solution)/shard_map/ppermute | solution.py:313
  21.3 8.6 %collective-permute-start.2 = (bf16[16,2048]{1,0:T(8,128)(2,1)S(1)}, bf16[16,2048]{1,0:T(8,128)(2,1)S(1)}, u32[]{:S(2)}, u32[]{:S(2)}) collective-permute-start(bf16[16,2048]{1,0:T(8,128)(2,1)S(1)} %get-tuple-element.40), channel_id=1, source_target_pairs={{0,4},{2,6},{4,0},{6,2},{1,5},{3,7},{5,1},{7,3},{8,12},{10,14},{12... | collective-permute-start | bytes 196616 | tf_op jit(solution)/shard_map/ppermute | solution.py:313
  23.7 6.2 %collective-permute-start.3 = (bf16[16,2048]{1,0:T(8,128)(2,1)S(1)}, bf16[16,2048]{1,0:T(8,128)(2,1)S(1)}, u32[]{:S(2)}, u32[]{:S(2)}) collective-permute-start(bf16[16,2048]{1,0:T(8,128)(2,1)S(1)} %get-tuple-element.41), channel_id=1, source_target_pairs={{0,6},{2,0},{4,2},{6,4},{1,7},{3,1},{5,3},{7,5},{8,14},{10,8},{12,... | collective-permute-start | bytes 196616 | tf_op jit(solution)/shard_map/ppermute | solution.py:313
  29.9 3.3 %collective-permute-start.4 = (f32[768,128]{1,0:T(8,128)S(1)}, f32[768,128]{1,0:T(8,128)S(1)}, u32[]{:S(2)}, u32[]{:S(2)}) collective-permute-start(f32[768,128]{1,0:T(8,128)S(1)} %get-tuple-element.47), channel_id=1, source_target_pairs={{0,8},{8,0},{1,9},{9,1},{2,10},{10,2},{3,11},{11,3},{4,12},{12,4},... | collective-permute-start | bytes 1179656 | tf_op jit(solution)/shard_map/ppermute | solution.py:328
  33.9 11.9 %all-to-all-start.1 = ((bf16[16,48,128]{2,1,0:T(8,128)(2,1)}), bf16[16,48,128]{2,1,0:T(8,128)(2,1)S(1)}, u32[]{:S(2)}, u32[]{:S(2)}) async-start(bf16[16,48,128]{2,1,0:T(8,128)(2,1)} %bitcast.3), calls=%async_computation.1 | async-start | bytes 393216 | tf_op jit(solution)/shard_map/all_to_all | solution.py:277
  38.8 21.8 %collective-permute-start.5 = (bf16[4,8,3072]{2,1,0:T(8,128)(2,1)S(1)}, bf16[4,8,3072]{2,1,0:T(8,128)(2,1)S(1)}, u32[]{:S(2)}, u32[]{:S(2)}) collective-permute-start(bf16[4,8,3072]{2,1,0:T(8,128)(2,1)S(1)} %get-tuple-element.50), channel_id=1, source_target_pairs={{0,1},{1,0},{2,3},{3,2},{4,5},{5,4},{6,7},{7,6},{8,9},{9,8},{10,11... | collective-permute-start | bytes 589832 | tf_op jit(solution)/shard_map/ppermute | solution.py:336
  73.2 3.6 %collective-permute-start.6 = (bf16[768,128]{1,0:T(8,128)(2,1)S(1)}, bf16[768,128]{1,0:T(8,128)(2,1)S(1)}, u32[]{:S(2)}, u32[]{:S(2)}) collective-permute-start(bf16[768,128]{1,0:T(8,128)(2,1)S(1)} %bitcast.10), channel_id=1, source_target_pairs={{0,8},{8,0},{1,9},{9,1},{2,10},{10,2},{3,11},{11,3},{4,12},{12,4},... | collective-permute-start | bytes 589832 | tf_op jit(solution)/shard_map/ppermute | solution.py:340

commit v4 on v3

--- a/solution.py
+++ b/solution.py
@@ -194,14 +194,23 @@
     outer = jnp.concatenate([u_ref[...], zero_ref[...]], axis=1)
     first = lax.dot_general(outer, grad_pre, across, preferred_element_type=F)
     rest = lax.dot_general(rest_ref[...], grad_pre, across, preferred_element_type=F)
-    both[0:576, :] = second[:, 0:128]
-    both[576:864, :] = jnp.concatenate([second[0:288, 128:192], second[288:576, 128:192]], axis=1)
-    both[864:1008, :] = jnp.concatenate([first[0:144, :], first[144:288, :]], axis=1)
-    both[1008:1296, :] = jnp.concatenate([rest[0:288, :], rest[288:576, :]], axis=1)
-    both[1296:ROWS, :] = jnp.zeros((ROWS - 1296, 128), F)
+    one = jnp.concatenate([first, rest], axis=0)
+    back, same, ahead = (second[:, a * C1 : (a + 1) * C1] for a in range(3))
+    for half, (left, right) in enumerate(
+        (
+            ([back[0:432]], [back[432:576], same[0:288]]),
+            ([same[288:576], ahead[0:144]], [ahead[144:576]]),
+        )
+    ):
+        at = half * HALF
+        left, right = (jnp.concatenate(side, axis=0) if len(side) > 1 else side[0] for side in (left, right))
+        both[at : at + 432, :] = jnp.concatenate([left, right], axis=1)
+        start = half * 432
+        both[at + 432 : at + 648, :] = jnp.concatenate([one[start : start + 216], one[start + 216 : start + 432]], axis=1)
+        both[at + 648 : at + HALF, :] = jnp.zeros((HALF - 648, 128), F)
     core = lax.axis_index("core")
     mine_ref[...] = both[pl.ds(pl.multiple_of(core * HALF, HALF), HALF), :]
-    other_ref[...] = both[pl.ds(pl.multiple_of((1 - core) * HALF, HALF), HALF), :]
+    other_ref[...] = both[pl.ds(pl.multiple_of((1 - core) * HALF, HALF), HALF), :].astype(BF)
 
 
 def split_sides(own_ref, one_ref, two_ref, three_ref, keep_ref, send_ref):
@@ -244,18 +253,15 @@
         o_ref[at] = total
 
 
-def unpack_gradients(mine_ref, other_ref, one_ref, two_ref, both):
+def unpack_gradients(mine_ref, other_ref, one_ref, two_ref):
     core = lax.axis_index("core")
-    both[pl.ds(pl.multiple_of(core * HALF, HALF), HALF), :] = mine_ref[...].astype(F)
-    both[pl.ds(pl.multiple_of((1 - core) * HALF, HALF), HALF), :] = other_ref[...].astype(F)
-    two_ref[0:576, :] = both[0:576, 0:64]
-    two_ref[576:1152, :] = both[0:576, 64:128]
-    two_ref[1152:1440, :] = both[576:864, 0:64]
-    two_ref[1440:1728, :] = both[576:864, 64:128]
-    one_ref[0:144, :] = both[864:1008, 0:64]
-    one_ref[144:288, :] = both[864:1008, 64:128]
-    one_ref[288:576, :] = both[1008:1296, 0:64]
-    one_ref[576:864, :] = both[1008:1296, 64:128]
+    for half, ref in ((core, mine_ref), (1 - core, other_ref)):
+        value = ref[...].astype(F)
+        two, one = pl.multiple_of(half * 864, 8), pl.multiple_of(half * 432, 8)
+        two_ref[pl.ds(two, 432), :] = value[0:432, 0:64]
+        two_ref[pl.ds(two + 432, 432), :] = value[0:432, 64:128]
+        one_ref[pl.ds(one, 216), :] = value[432:648, 0:64]
+        one_ref[pl.ds(one + 216, 216), :] = value[432:648, 64:128]
 
 
 def sds(shape, dtype):
@@ -314,7 +320,7 @@
     ]
     mine, other = call(
         gradients,
-        [sds((HALF, 128), F), sds((HALF, 128), F)],
+        [sds((HALF, 128), F), sds((HALF, 128), BF)],
         [pltpu.VMEM((3 * C1, SLAB), BF), pltpu.VMEM((9 * C1, SLAB), BF), pltpu.VMEM((ROWS, 128), F)],
         FLOPS_GRAD,
         COST_GRAD,
@@ -325,7 +331,7 @@
     keep, send = call(split_sides, [sds((4, 8, 4 * CELLS), F), sds((4, 8, 6 * CELLS), BF)], [], 0, 10000)(
         sent[0], *arrived
     )
-    chip = mine + lax.ppermute(other, "core", pairs)
+    chip = mine + lax.ppermute(other, "core", pairs).astype(F)
     chip, send = lax.optimization_barrier((chip.astype(SENT), send))
     count = lax.axis_size("x") * lax.axis_size("y")
     deep = lax.axis_size("zl") * lax.axis_size("zh")
@@ -341,7 +347,7 @@
     total_one, total_two = call(
         unpack_gradients,
         [sds((27 * C0, C1), F), sds((27 * C1, C1), F)],
-        [pltpu.VMEM((ROWS, 128), F)],
+        (),
         FLOPS_LAST,
         4000000,
     )(my_half, other_half)

time: 78.5 us -> 78.1 us (level)
  no operation moved by 1% of the time
where the time goes in v4:
time: 78.1 us; the launch traced here: 77.8 us
  starting transfers between devices  33.7 us (43%)
  blocking collectives  27.2 us (35%)
  Pallas kernels  9.7 us (12%)
  waiting for transfers between devices  5.63 us (7%)
    all_to_all x2, blocking collectives, exchange(): return lax.all_to_all(value, axes, split_axis=0, concat_axis=0, tiled=True)  27.2 us
    ppermute x1, starting transfers between devices, along(): return lax.ppermute(value, SPACE, pairs)  9.65 us
    all_to_all x2, starting transfers between devices, exchange(): return lax.all_to_all(value, axes, split_axis=0, concat_axis=0, tiled=True)  9.03 us
    ppermute x1, starting transfers between devices, shards(): got = lax.ppermute(send, 'zh', [(0, 1), (1, 0)])  5.44 us
    ppermute x3, starting transfers between devices, shards(): lax.ppermute(sent[step], 'y', [(at, (at + step) % 4) for at in range(4)])  5.11 us
    all_to_all x2, waiting for transfers between devices, exchange(): return lax.all_to_all(value, axes, split_axis=0, concat_axis=0, tiled=True)  4.6 us
    ppermute x1, starting transfers between devices, shards(): other_half = lax.ppermute(my_half, 'core', pairs)  2.45 us
    pallas_call x1, Pallas kernels, shards(): call(pack_inputs, [sds((8, 8, 2048), BF), sds((1, C0, 1, 16, 128), BF)],...  2.12 us
  transfers between devices with their start and end apart: 9, of which 3 were waited for; matrix products, arithmetic and copies ran while one was open for 0% of the time, Pallas kernels for 8%

profile of v4, /device:TPU:1, one launch (start us, length us, event | category | flops | bytes accessed | tf_op | source)
XLA Modules:
  0.0 77.8 jit_solution(18104487018898301687)
XLA Ops:
  0.6 0.0 copy-start
  0.6 0.0 copy-start.1
  0.7 0.0 copy-start.2
  0.7 2.1 %shard_map.67 = (bf16[8,8,2048]{2,1,0:T(8,128)(2,1)}, bf16[1,32,1,16,128]{4,3,2,1,0:T(8,128)(2,1)}) custom-call(bf16[1,8,16,8,64]{4,3,2,1,0:T(8,128)(2,1)} %x_ref.1, bf16[1,32,4,16,128]{4,3,2,1,0:T(8,128)(2,1)} %v_ref.3), custom_call_target="tpu_custom_call" | custom-call | bytes 4000000 | tf_op jit(solution)/shard_map/pallas_call | solution.py:291
  2.8 9.6 %collective-permute-start = (bf16[1,32,1,16,128]{4,3,2,1,0:T(8,128)(2,1)}, bf16[1,32,1,16,128]{4,3,2,1,0:T(8,128)(2,1)S(1)}, u32[]{:S(2)}, u32[]{:S(2)}) collective-permute-start(bf16[1,32,1,16,128]{4,3,2,1,0:T(8,128)(2,1)} %get-tuple-element.29), channel_id=1, source_target_pairs={{0,1},{1,2},{2,3},{3,4},{4,5},{5,6},{6,7},{8,9},{9,10},{10,11},{11... | collective-permute-start | bytes 393224 | tf_op jit(solution)/shard_map/ppermute | solution.py:279
  12.4 4.2 %all-to-all-start = ((bf16[8,8,2048]{2,1,0:T(8,128)(2,1)}), bf16[8,8,2048]{2,1,0:T(8,128)(2,1)S(1)}, u32[]{:S(2)}, u32[]{:S(2)}) async-start(bf16[8,8,2048]{2,1,0:T(8,128)(2,1)} %get-tuple-element.37), calls=%async_computation | async-start | bytes 524288 | tf_op jit(solution)/shard_map/all_to_all | solution.py:283
  16.6 0.0 copy-done
  16.7 1.3 %shard_map.68 = (bf16[288,512]{1,0:T(8,128)(2,1)S(1)}, bf16[576,1024]{1,0:T(8,128)(2,1)S(1)}, bf16[864,64]{1,0:T(8,128)(2,1)S(1)}, bf16[576,192]{1,0:T(8,128)(2,1)S(1)}) custom-call(bf16[1,32,4,16,128]{4,3,2,1,0:T(8,128)(2,1)S(1)} %copy-done, bf16[864,64]{1,0:T(8,128)(2,1)S(1)} %bitcast.9, bf16[1728,64]{1,0:T(8,128)(2,1)S(1)} %bitcast.8), custom_call_target="tpu_custom_call" | custom-call | bytes 12000000 | tf_op jit(solution)/shard_map/pallas_call | solution.py:303
  18.0 0.0 collective-permute-done.h_ref
  18.0 1.7 %shard_map.69 = (bf16[288,512]{1,0:T(8,128)(2,1)S(1)}, bf16[64,1024]{1,0:T(8,128)(2,1)S(1)}, f32[16,2048]{1,0:T(8,128)S(1)}, bf16[16,2048]{1,0:T(8,128)(2,1)S(1)...) custom-call(bf16[1,32,1,16,128]{4,3,2,1,0:T(8,128)(2,1)S(1)} %collective-permute-done.h_ref, ...), custom_call_target="tpu_custom_call" | custom-call | flops 10000000000 | bytes 8000000 | tf_op jit(solution)/shard_map/pallas_call | solution.py:311
  19.7 1.5 %collective-permute-start.1 = (bf16[16,2048]{1,0:T(8,128)(2,1)S(1)}, bf16[16,2048]{1,0:T(8,128)(2,1)S(1)}, u32[]{:S(2)}, u32[]{:S(2)}) collective-permute-start(bf16[16,2048]{1,0:T(8,128)(2,1)S(1)} %get-tuple-element.39), channel_id=1, source_target_pairs={{0,2},{2,4},{4,6},{6,0},{1,3},{3,5},{5,7},{7,1},{8,10},{10,12},{12... | collective-permute-start | bytes 196616 | tf_op jit(solution)/shard_map/ppermute | solution.py:319
  21.3 2.4 %collective-permute-start.2 = (bf16[16,2048]{1,0:T(8,128)(2,1)S(1)}, bf16[16,2048]{1,0:T(8,128)(2,1)S(1)}, u32[]{:S(2)}, u32[]{:S(2)}) collective-permute-start(bf16[16,2048]{1,0:T(8,128)(2,1)S(1)} %get-tuple-element.40), channel_id=1, source_target_pairs={{0,4},{2,6},{4,0},{6,2},{1,5},{3,7},{5,1},{7,3},{8,12},{10,14},{12... | collective-permute-start | bytes 196616 | tf_op jit(solution)/shard_map/ppermute | solution.py:319
  23.7 1.2 %collective-permute-start.3 = (bf16[16,2048]{1,0:T(8,128)(2,1)S(1)}, bf16[16,2048]{1,0:T(8,128)(2,1)S(1)}, u32[]{:S(2)}, u32[]{:S(2)}) collective-permute-start(bf16[16,2048]{1,0:T(8,128)(2,1)S(1)} %get-tuple-element.41), channel_id=1, source_target_pairs={{0,6},{2,0},{4,2},{6,4},{1,7},{3,1},{5,3},{7,5},{8,14},{10,8},{12,... | collective-permute-start | bytes 196616 | tf_op jit(solution)/shard_map/ppermute | solution.py:319
  24.8 3.0 %all-to-all-done = bf16[8,8,2048]{2,1,0:T(8,128)(2,1)S(1)} async-done(((bf16[8,8,2048]{2,1,0:T(8,128)(2,1)}), bf16[8,8,2048]{2,1,0:T(8,128)(2,1)S(1)}, u32[]{:S(2)}, u32[]{:S(2)}) %all-to-all-start) | async-done | bytes 262176 | tf_op jit(solution)/shard_map/all_to_all | solution.py:283
  27.8 2.1 %shard_map.70 = (f32[768,128]{1,0:T(8,128)S(1)}, bf16[768,128]{1,0:T(8,128)(2,1)S(1)}) custom-call(bf16[288,512]{1,0:T(8,128)(2,1)S(1)} %get-tuple-element.35.u_ref, bf16[288,512]{1,0:T(8,128)(2,1)S(1)} %get-tuple-element.30.zero_ref, bf16[576,1024]{1,0:T(8,128)(2,1)S(1)} %get-tuple-element.31.rest_ref, bf16[64,1024]{1,0:T(8,128)(2,1)S(1)} %get-tuple-element.36.act_ref, ...), custom_call_target="tpu_custom_call" | custom-call | bytes 12000000 | tf_op jit(solution)/shard_map/pallas_call | solution.py:321
  29.9 0.0 collective-permute-done.1.one_ref
  29.9 0.0 collective-permute-done.2.two_ref
  29.9 0.0 collective-permute-done.3.three_ref
  29.9 2.0 %collective-permute-start.4 = (bf16[768,128]{1,0:T(8,128)(2,1)S(1)}, bf16[768,128]{1,0:T(8,128)(2,1)S(1)}, u32[]{:S(2)}, u32[]{:S(2)}) collective-permute-start(bf16[768,128]{1,0:T(8,128)(2,1)S(1)} %get-tuple-element.47), channel_id=1, source_target_pairs={{0,8},{8,0},{1,9},{9,1},{2,10},{10,2},{3,11},{11,3},{4,12},{12,4},... | collective-permute-start | bytes 589832 | tf_op jit(solution)/shard_map/ppermute | solution.py:334
  31.9 0.1 shard_map.71
  32.0 1.0 %collective-permute-done.4 = bf16[768,128]{1,0:T(8,128)(2,1)S(1)} collective-permute-done((bf16[768,128]{1,0:T(8,128)(2,1)S(1)}, bf16[768,128]{1,0:T(8,128)(2,1)S(1)}, u32[]{:S(2)}, u32[]{:S(2)}) %collective-permute-start.4) | collective-permute-done | bytes 196640 | tf_op jit(solution)/shard_map/ppermute | solution.py:334
  33.0 0.7 add_convert_fusion
  33.7 4.8 %all-to-all-start.1 = ((bf16[16,48,128]{2,1,0:T(8,128)(2,1)}), bf16[16,48,128]{2,1,0:T(8,128)(2,1)S(1)}, u32[]{:S(2)}, u32[]{:S(2)}) async-start(bf16[16,48,128]{2,1,0:T(8,128)(2,1)} %bitcast.3), calls=%async_computation.1 | async-start | bytes 393216 | tf_op jit(solution)/shard_map/all_to_all | solution.py:283
  38.6 5.4 %collective-permute-start.5 = (bf16[4,8,3072]{2,1,0:T(8,128)(2,1)S(1)}, bf16[4,8,3072]{2,1,0:T(8,128)(2,1)S(1)}, u32[]{:S(2)}, u32[]{:S(2)}) collective-permute-start(bf16[4,8,3072]{2,1,0:T(8,128)(2,1)S(1)} %get-tuple-element.50), channel_id=1, source_target_pairs={{0,1},{1,0},{2,3},{3,2},{4,5},{5,4},{6,7},{7,6},{8,9},{9,8},{10,11... | collective-permute-start | bytes 589832 | tf_op jit(solution)/shard_map/ppermute | solution.py:342
  44.0 1.6 %all-to-all-done.1.x_ref = bf16[16,48,128]{2,1,0:T(8,128)(2,1)S(1)} async-done(((bf16[16,48,128]{2,1,0:T(8,128)(2,1)}), bf16[16,48,128]{2,1,0:T(8,128)(2,1)S(1)}, u32[]{:S(2)}, u32[]{:S(2)}) %all-to-all-start.1) | async-done | bytes 196640 | tf_op jit(solution)/shard_map/all_to_all | solution.py:283
  45.7 14.6 %all_to_all.20.x_ref = bf16[8,48,128]{2,1,0:T(8,128)(2,1)S(1)} all-to-all(bf16[8,48,128]{2,1,0:T(8,128)(2,1)S(1)} %shard_map.72), channel_id=1, replica_groups=mesh['zl'=4,'x'=4,'core'=2,'y'=4,'zh'=2] {'zl','zh'}, dimensions={0} | all-to-all | bytes 196608 | tf_op jit(solution)/shard_map/all_to_all | solution.py:283
  60.3 0.0 collective-permute-done.5.got_ref
  60.3 12.7 %all_to_all.21 = bf16[16,48,128]{2,1,0:T(8,128)(2,1)S(1)} all-to-all(bf16[16,48,128]{2,1,0:T(8,128)(2,1)S(1)} %shard_map.73), channel_id=1, replica_groups=mesh['zl'=4,'x'=4,'core'=2,'y'=4,'zh'=2] {'x','y'}, dimensions={0} | all-to-all | bytes 393216 | tf_op jit(solution)/shard_map/all_to_all | solution.py:283
  72.9 2.4 %collective-permute-start.6 = (bf16[768,128]{1,0:T(8,128)(2,1)S(1)}, bf16[768,128]{1,0:T(8,128)(2,1)S(1)}, u32[]{:S(2)}, u32[]{:S(2)}) collective-permute-start(bf16[768,128]{1,0:T(8,128)(2,1)S(1)} %bitcast.10), channel_id=1, source_target_pairs={{0,8},{8,0},{1,9},{9,1},{2,10},{10,2},{3,11},{11,3},{4,12},{12,4},... | collective-permute-start | bytes 589832 | tf_op jit(solution)/shard_map/ppermute | solution.py:346
  75.4 1.1 %shard_map.74 = bf16[1,8,16,8,64]{4,3,2,1,0:T(8,128)(2,1)} custom-call(f32[4,8,2048]{2,1,0:T(8,128)S(1)} %get-tuple-element.45.keep_ref, bf16[4,8,3072]{2,1,0:T(8,128)(2,1)S(1)} %collective-permute-done.5.got_ref), custom_call_target="tpu_custom_call" | custom-call | bytes 10000 | tf_op jit(solution)/shard_map/pallas_call | solution.py:354
  76.5 0.0 collective-permute-done.6.other_ref
  76.5 1.2 %shard_map.75 = (f32[864,64]{1,0:T(8,128)}, f32[1728,64]{1,0:T(8,128)}) custom-call(bf16[768,128]{1,0:T(8,128)(2,1)S(1)} %bitcast.11, bf16[768,128]{1,0:T(8,128)(2,1)S(1)} %collective-permute-done.6.other_ref), custom_call_target="tpu_custom_call" | custom-call | flops 2000000000 | bytes 4000000 | tf_op jit(solution)/shard_map/pallas_call | solution.py:347
  (4 shorter events, 0.1 us)
Async XLA Ops:
  0.6 16.0 %copy-start = (bf16[1,32,4,16,128]{4,3,2,1,0:T(8,128)(2,1)S(1)}, bf16[1,32,4,16,128]{4,3,2,1,0:T(8,128)(2,1)}, u32[]{:S(2)}) copy-start(bf16[1,32,4,16,128]{4,3,2,1,0:T(8,128)(2,1)} %v_ref.3) | copy-start | bytes 1572868
  0.6 16.0 %copy-start.1 = (bf16[27,64,64]{2,1,0:T(8,128)(2,1)S(1)}, bf16[27,64,64]{2,1,0:T(8,128)(2,1)}, u32[]{:S(2)}) copy-start(bf16[27,64,64]{2,1,0:T(8,128)(2,1)} %param.6) | copy-start | bytes 663556
  0.7 16.0 %copy-start.2 = (bf16[27,32,64]{2,1,0:T(8,128)(2,1)S(1)}, bf16[27,32,64]{2,1,0:T(8,128)(2,1)}, u32[]{:S(2)}) copy-start(bf16[27,32,64]{2,1,0:T(8,128)(2,1)} %param.5) | copy-start | bytes 331780
  2.8 15.2 %collective-permute-start = (bf16[1,32,1,16,128]{4,3,2,1,0:T(8,128)(2,1)}, bf16[1,32,1,16,128]{4,3,2,1,0:T(8,128)(2,1)S(1)}, u32[]{:S(2)}, u32[]{:S(2)}) collective-permute-start(bf16[1,32,1,16,128]{4,3,2,1,0:T(8,128)(2,1)} %get-tuple-element.29), channel_id=1, source_target_pairs={{0,1},{1,2},{2,3},{3,4},{4,5},{5,6},{6,7},{8,9},{9,10},{10,11},{11... | collective-permute-start | bytes 393224 | tf_op jit(solution)/shard_map/ppermute | solution.py:279
  12.4 15.4 %all-to-all-start = ((bf16[8,8,2048]{2,1,0:T(8,128)(2,1)}), bf16[8,8,2048]{2,1,0:T(8,128)(2,1)S(1)}, u32[]{:S(2)}, u32[]{:S(2)}) async-start(bf16[8,8,2048]{2,1,0:T(8,128)(2,1)} %get-tuple-element.37), calls=%async_computation | async-start | bytes 524288 | tf_op jit(solution)/shard_map/all_to_all | solution.py:283
  19.7 10.2 %collective-permute-start.1 = (bf16[16,2048]{1,0:T(8,128)(2,1)S(1)}, bf16[16,2048]{1,0:T(8,128)(2,1)S(1)}, u32[]{:S(2)}, u32[]{:S(2)}) collective-permute-start(bf16[16,2048]{1,0:T(8,128)(2,1)S(1)} %get-tuple-element.39), channel_id=1, source_target_pairs={{0,2},{2,4},{4,6},{6,0},{1,3},{3,5},{5,7},{7,1},{8,10},{10,12},{12... | collective-permute-start | bytes 196616 | tf_op jit(solution)/shard_map/ppermute | solution.py:319
  21.3 8.7 %collective-permute-start.2 = (bf16[16,2048]{1,0:T(8,128)(2,1)S(1)}, bf16[16,2048]{1,0:T(8,128)(2,1)S(1)}, u32[]{:S(2)}, u32[]{:S(2)}) collective-permute-start(bf16[16,2048]{1,0:T(8,128)(2,1)S(1)} %get-tuple-element.40), channel_id=1, source_target_pairs={{0,4},{2,6},{4,0},{6,2},{1,5},{3,7},{5,1},{7,3},{8,12},{10,14},{12... | collective-permute-start | bytes 196616 | tf_op jit(solution)/shard_map/ppermute | solution.py:319
  23.7 6.3 %collective-permute-start.3 = (bf16[16,2048]{1,0:T(8,128)(2,1)S(1)}, bf16[16,2048]{1,0:T(8,128)(2,1)S(1)}, u32[]{:S(2)}, u32[]{:S(2)}) collective-permute-start(bf16[16,2048]{1,0:T(8,128)(2,1)S(1)} %get-tuple-element.41), channel_id=1, source_target_pairs={{0,6},{2,0},{4,2},{6,4},{1,7},{3,1},{5,3},{7,5},{8,14},{10,8},{12,... | collective-permute-start | bytes 196616 | tf_op jit(solution)/shard_map/ppermute | solution.py:319
  29.9 3.1 %collective-permute-start.4 = (bf16[768,128]{1,0:T(8,128)(2,1)S(1)}, bf16[768,128]{1,0:T(8,128)(2,1)S(1)}, u32[]{:S(2)}, u32[]{:S(2)}) collective-permute-start(bf16[768,128]{1,0:T(8,128)(2,1)S(1)} %get-tuple-element.47), channel_id=1, source_target_pairs={{0,8},{8,0},{1,9},{9,1},{2,10},{10,2},{3,11},{11,3},{4,12},{12,4},... | collective-permute-start | bytes 589832 | tf_op jit(solution)/shard_map/ppermute | solution.py:334
  33.7 11.9 %all-to-all-start.1 = ((bf16[16,48,128]{2,1,0:T(8,128)(2,1)}), bf16[16,48,128]{2,1,0:T(8,128)(2,1)S(1)}, u32[]{:S(2)}, u32[]{:S(2)}) async-start(bf16[16,48,128]{2,1,0:T(8,128)(2,1)} %bitcast.3), calls=%async_computation.1 | async-start | bytes 393216 | tf_op jit(solution)/shard_map/all_to_all | solution.py:283
  38.6 21.7 %collective-permute-start.5 = (bf16[4,8,3072]{2,1,0:T(8,128)(2,1)S(1)}, bf16[4,8,3072]{2,1,0:T(8,128)(2,1)S(1)}, u32[]{:S(2)}, u32[]{:S(2)}) collective-permute-start(bf16[4,8,3072]{2,1,0:T(8,128)(2,1)S(1)} %get-tuple-element.50), channel_id=1, source_target_pairs={{0,1},{1,0},{2,3},{3,2},{4,5},{5,4},{6,7},{7,6},{8,9},{9,8},{10,11... | collective-permute-start | bytes 589832 | tf_op jit(solution)/shard_map/ppermute | solution.py:342
  72.9 3.6 %collective-permute-start.6 = (bf16[768,128]{1,0:T(8,128)(2,1)S(1)}, bf16[768,128]{1,0:T(8,128)(2,1)S(1)}, u32[]{:S(2)}, u32[]{:S(2)}) collective-permute-start(bf16[768,128]{1,0:T(8,128)(2,1)S(1)} %bitcast.10), channel_id=1, source_target_pairs={{0,8},{8,0},{1,9},{9,1},{2,10},{10,2},{3,11},{11,3},{4,12},{12,4},... | collective-permute-start | bytes 589832 | tf_op jit(solution)/shard_map/ppermute | solution.py:346

commit v5 on v4

--- a/solution.py
+++ b/solution.py
@@ -221,7 +221,7 @@
         first, second = value[0:8], value[8:16]
         keep_ref[source] = jnp.where(lower, first, second)
         send_ref[source, :, 0 : 4 * CELLS] = jnp.where(lower, second, first).astype(BF)
-        send_ref[source, :, 4 * CELLS :] = jnp.zeros((8, 2 * CELLS), BF)
+        send_ref[source, :, 4 * CELLS :] = jnp.zeros((8, 768), BF)
 
 
 def unpack_features(keep_ref, got_ref, o_ref, slabs, flat):
@@ -328,7 +328,7 @@
     cores = lax.axis_size("core")
     pairs = [(at, at ^ 1) for at in range(cores)]
     other, arrived = lax.optimization_barrier((other, arrived))
-    keep, send = call(split_sides, [sds((4, 8, 4 * CELLS), F), sds((4, 8, 6 * CELLS), BF)], [], 0, 10000)(
+    keep, send = call(split_sides, [sds((4, 8, 4 * CELLS), F), sds((4, 8, 2816), BF)], [], 0, 10000)(
         sent[0], *arrived
     )
     chip = mine + lax.ppermute(other, "core", pairs).astype(F)

time: 78.1 us -> 77.7 us (level)
  blocking collectives: 27.2 us -> 26.1 us
    all_to_all x2, blocking collectives: 27.2 us -> 26.1 us  [exchange(): return lax.all_to_all(value, axes, split_axis=0, concat_axis=0, tiled=True)]
where the time goes in v5:
time: 77.7 us; the launch traced here: 77.4 us
  starting transfers between devices  34.4 us (44%)
  blocking collectives  26.1 us (34%)
  Pallas kernels  9.7 us (12%)
  waiting for transfers between devices  5.63 us (7%)
    all_to_all x2, blocking collectives, exchange(): return lax.all_to_all(value, axes, split_axis=0, concat_axis=0, tiled=True)  26.1 us
    ppermute x1, starting transfers between devices, along(): return lax.ppermute(value, SPACE, pairs)  9.65 us
    all_to_all x2, starting transfers between devices, exchange(): return lax.all_to_all(value, axes, split_axis=0, concat_axis=0, tiled=True)  9.03 us
    ppermute x1, starting transfers between devices, shards(): got = lax.ppermute(send, 'zh', [(0, 1), (1, 0)])  5.44 us
    ppermute x3, starting transfers between devices, shards(): lax.ppermute(sent[step], 'y', [(at, (at + step) % 4) for at in range(4)])  5.11 us
    all_to_all x2, waiting for transfers between devices, exchange(): return lax.all_to_all(value, axes, split_axis=0, concat_axis=0, tiled=True)  4.6 us
    ppermute x1, starting transfers between devices, shards(): other_half = lax.ppermute(my_half, 'core', pairs)  3.21 us
    pallas_call x1, Pallas kernels, shards(): call(pack_inputs, [sds((8, 8, 2048), BF), sds((1, C0, 1, 16, 128), BF)],...  2.12 us
  transfers between devices with their start and end apart: 9, of which 3 were waited for; matrix products, arithmetic and copies ran while one was open for 0% of the time, Pallas kernels for 8%

profile of v5, /device:TPU:1, one launch (start us, length us, event | category | flops | bytes accessed | tf_op | source)
XLA Modules:
  0.0 77.4 jit_solution(14952016178784885998)
XLA Ops:
  0.6 0.0 copy-start
  0.6 0.0 copy-start.1
  0.7 0.0 copy-start.2
  0.7 2.1 %shard_map.67 = (bf16[8,8,2048]{2,1,0:T(8,128)(2,1)}, bf16[1,32,1,16,128]{4,3,2,1,0:T(8,128)(2,1)}) custom-call(bf16[1,8,16,8,64]{4,3,2,1,0:T(8,128)(2,1)} %x_ref.1, bf16[1,32,4,16,128]{4,3,2,1,0:T(8,128)(2,1)} %v_ref.3), custom_call_target="tpu_custom_call" | custom-call | bytes 4000000 | tf_op jit(solution)/shard_map/pallas_call | solution.py:291
  2.8 9.6 %collective-permute-start = (bf16[1,32,1,16,128]{4,3,2,1,0:T(8,128)(2,1)}, bf16[1,32,1,16,128]{4,3,2,1,0:T(8,128)(2,1)S(1)}, u32[]{:S(2)}, u32[]{:S(2)}) collective-permute-start(bf16[1,32,1,16,128]{4,3,2,1,0:T(8,128)(2,1)} %get-tuple-element.29), channel_id=1, source_target_pairs={{0,1},{1,2},{2,3},{3,4},{4,5},{5,6},{6,7},{8,9},{9,10},{10,11},{11... | collective-permute-start | bytes 393224 | tf_op jit(solution)/shard_map/ppermute | solution.py:279
  12.4 4.2 %all-to-all-start = ((bf16[8,8,2048]{2,1,0:T(8,128)(2,1)}), bf16[8,8,2048]{2,1,0:T(8,128)(2,1)S(1)}, u32[]{:S(2)}, u32[]{:S(2)}) async-start(bf16[8,8,2048]{2,1,0:T(8,128)(2,1)} %get-tuple-element.37), calls=%async_computation | async-start | bytes 524288 | tf_op jit(solution)/shard_map/all_to_all | solution.py:283
  16.6 0.0 copy-done
  16.7 1.3 %shard_map.68 = (bf16[288,512]{1,0:T(8,128)(2,1)S(1)}, bf16[576,1024]{1,0:T(8,128)(2,1)S(1)}, bf16[864,64]{1,0:T(8,128)(2,1)S(1)}, bf16[576,192]{1,0:T(8,128)(2,1)S(1)}) custom-call(bf16[1,32,4,16,128]{4,3,2,1,0:T(8,128)(2,1)S(1)} %copy-done, bf16[864,64]{1,0:T(8,128)(2,1)S(1)} %bitcast.9, bf16[1728,64]{1,0:T(8,128)(2,1)S(1)} %bitcast.8), custom_call_target="tpu_custom_call" | custom-call | bytes 12000000 | tf_op jit(solution)/shard_map/pallas_call | solution.py:303
  18.0 0.0 collective-permute-done.h_ref
  18.0 1.7 %shard_map.69 = (bf16[288,512]{1,0:T(8,128)(2,1)S(1)}, bf16[64,1024]{1,0:T(8,128)(2,1)S(1)}, f32[16,2048]{1,0:T(8,128)S(1)}, bf16[16,2048]{1,0:T(8,128)(2,1)S(1)...) custom-call(bf16[1,32,1,16,128]{4,3,2,1,0:T(8,128)(2,1)S(1)} %collective-permute-done.h_ref, ...), custom_call_target="tpu_custom_call" | custom-call | flops 10000000000 | bytes 8000000 | tf_op jit(solution)/shard_map/pallas_call | solution.py:311
  19.7 1.5 %collective-permute-start.1 = (bf16[16,2048]{1,0:T(8,128)(2,1)S(1)}, bf16[16,2048]{1,0:T(8,128)(2,1)S(1)}, u32[]{:S(2)}, u32[]{:S(2)}) collective-permute-start(bf16[16,2048]{1,0:T(8,128)(2,1)S(1)} %get-tuple-element.39), channel_id=1, source_target_pairs={{0,2},{2,4},{4,6},{6,0},{1,3},{3,5},{5,7},{7,1},{8,10},{10,12},{12... | collective-permute-start | bytes 196616 | tf_op jit(solution)/shard_map/ppermute | solution.py:319
  21.3 2.4 %collective-permute-start.2 = (bf16[16,2048]{1,0:T(8,128)(2,1)S(1)}, bf16[16,2048]{1,0:T(8,128)(2,1)S(1)}, u32[]{:S(2)}, u32[]{:S(2)}) collective-permute-start(bf16[16,2048]{1,0:T(8,128)(2,1)S(1)} %get-tuple-element.40), channel_id=1, source_target_pairs={{0,4},{2,6},{4,0},{6,2},{1,5},{3,7},{5,1},{7,3},{8,12},{10,14},{12... | collective-permute-start | bytes 196616 | tf_op jit(solution)/shard_map/ppermute | solution.py:319
  23.7 1.2 %collective-permute-start.3 = (bf16[16,2048]{1,0:T(8,128)(2,1)S(1)}, bf16[16,2048]{1,0:T(8,128)(2,1)S(1)}, u32[]{:S(2)}, u32[]{:S(2)}) collective-permute-start(bf16[16,2048]{1,0:T(8,128)(2,1)S(1)} %get-tuple-element.41), channel_id=1, source_target_pairs={{0,6},{2,0},{4,2},{6,4},{1,7},{3,1},{5,3},{7,5},{8,14},{10,8},{12,... | collective-permute-start | bytes 196616 | tf_op jit(solution)/shard_map/ppermute | solution.py:319
  24.8 3.0 %all-to-all-done = bf16[8,8,2048]{2,1,0:T(8,128)(2,1)S(1)} async-done(((bf16[8,8,2048]{2,1,0:T(8,128)(2,1)}), bf16[8,8,2048]{2,1,0:T(8,128)(2,1)S(1)}, u32[]{:S(2)}, u32[]{:S(2)}) %all-to-all-start) | async-done | bytes 262176 | tf_op jit(solution)/shard_map/all_to_all | solution.py:283
  27.8 2.1 %shard_map.70 = (f32[768,128]{1,0:T(8,128)S(1)}, bf16[768,128]{1,0:T(8,128)(2,1)S(1)}) custom-call(bf16[288,512]{1,0:T(8,128)(2,1)S(1)} %get-tuple-element.35.u_ref, bf16[288,512]{1,0:T(8,128)(2,1)S(1)} %get-tuple-element.30.zero_ref, bf16[576,1024]{1,0:T(8,128)(2,1)S(1)} %get-tuple-element.31.rest_ref, bf16[64,1024]{1,0:T(8,128)(2,1)S(1)} %get-tuple-element.36.act_ref, ...), custom_call_target="tpu_custom_call" | custom-call | bytes 12000000 | tf_op jit(solution)/shard_map/pallas_call | solution.py:321
  29.9 0.0 collective-permute-done.1.one_ref
  29.9 0.0 collective-permute-done.2.two_ref
  29.9 0.0 collective-permute-done.3.three_ref
  29.9 2.0 %collective-permute-start.4 = (bf16[768,128]{1,0:T(8,128)(2,1)S(1)}, bf16[768,128]{1,0:T(8,128)(2,1)S(1)}, u32[]{:S(2)}, u32[]{:S(2)}) collective-permute-start(bf16[768,128]{1,0:T(8,128)(2,1)S(1)} %get-tuple-element.47), channel_id=1, source_target_pairs={{0,8},{8,0},{1,9},{9,1},{2,10},{10,2},{3,11},{11,3},{4,12},{12,4},... | collective-permute-start | bytes 589832 | tf_op jit(solution)/shard_map/ppermute | solution.py:334
  31.9 0.1 shard_map.71
  32.0 1.0 %collective-permute-done.4 = bf16[768,128]{1,0:T(8,128)(2,1)S(1)} collective-permute-done((bf16[768,128]{1,0:T(8,128)(2,1)S(1)}, bf16[768,128]{1,0:T(8,128)(2,1)S(1)}, u32[]{:S(2)}, u32[]{:S(2)}) %collective-permute-start.4) | collective-permute-done | bytes 196640 | tf_op jit(solution)/shard_map/ppermute | solution.py:334
  33.0 0.7 add_convert_fusion
  33.7 4.8 %all-to-all-start.1 = ((bf16[16,48,128]{2,1,0:T(8,128)(2,1)}), bf16[16,48,128]{2,1,0:T(8,128)(2,1)S(1)}, u32[]{:S(2)}, u32[]{:S(2)}) async-start(bf16[16,48,128]{2,1,0:T(8,128)(2,1)} %bitcast.3), calls=%async_computation.1 | async-start | bytes 393216 | tf_op jit(solution)/shard_map/all_to_all | solution.py:283
  38.6 5.4 %collective-permute-start.5 = (bf16[4,8,2816]{2,1,0:T(8,128)(2,1)S(1)}, bf16[4,8,2816]{2,1,0:T(8,128)(2,1)S(1)}, u32[]{:S(2)}, u32[]{:S(2)}) collective-permute-start(bf16[4,8,2816]{2,1,0:T(8,128)(2,1)S(1)} %get-tuple-element.50), channel_id=1, source_target_pairs={{0,1},{1,0},{2,3},{3,2},{4,5},{5,4},{6,7},{7,6},{8,9},{9,8},{10,11... | collective-permute-start | bytes 540680 | tf_op jit(solution)/shard_map/ppermute | solution.py:342
  44.0 1.6 %all-to-all-done.1.x_ref = bf16[16,48,128]{2,1,0:T(8,128)(2,1)S(1)} async-done(((bf16[16,48,128]{2,1,0:T(8,128)(2,1)}), bf16[16,48,128]{2,1,0:T(8,128)(2,1)S(1)}, u32[]{:S(2)}, u32[]{:S(2)}) %all-to-all-start.1) | async-done | bytes 196640 | tf_op jit(solution)/shard_map/all_to_all | solution.py:283
  45.7 14.6 %all_to_all.20.x_ref = bf16[8,48,128]{2,1,0:T(8,128)(2,1)S(1)} all-to-all(bf16[8,48,128]{2,1,0:T(8,128)(2,1)S(1)} %shard_map.72), channel_id=1, replica_groups=mesh['zl'=4,'x'=4,'core'=2,'y'=4,'zh'=2] {'zl','zh'}, dimensions={0} | all-to-all | bytes 196608 | tf_op jit(solution)/shard_map/all_to_all | solution.py:283
  60.3 0.0 collective-permute-done.5.got_ref
  60.3 11.5 %all_to_all.21 = bf16[16,48,128]{2,1,0:T(8,128)(2,1)S(1)} all-to-all(bf16[16,48,128]{2,1,0:T(8,128)(2,1)S(1)} %shard_map.73), channel_id=1, replica_groups=mesh['zl'=4,'x'=4,'core'=2,'y'=4,'zh'=2] {'x','y'}, dimensions={0} | all-to-all | bytes 393216 | tf_op jit(solution)/shard_map/all_to_all | solution.py:283
  71.8 3.2 %collective-permute-start.6 = (bf16[768,128]{1,0:T(8,128)(2,1)S(1)}, bf16[768,128]{1,0:T(8,128)(2,1)S(1)}, u32[]{:S(2)}, u32[]{:S(2)}) collective-permute-start(bf16[768,128]{1,0:T(8,128)(2,1)S(1)} %bitcast.10), channel_id=1, source_target_pairs={{0,8},{8,0},{1,9},{9,1},{2,10},{10,2},{3,11},{11,3},{4,12},{12,4},... | collective-permute-start | bytes 589832 | tf_op jit(solution)/shard_map/ppermute | solution.py:346
  75.0 1.1 %shard_map.74 = bf16[1,8,16,8,64]{4,3,2,1,0:T(8,128)(2,1)} custom-call(f32[4,8,2048]{2,1,0:T(8,128)S(1)} %get-tuple-element.45.keep_ref, bf16[4,8,2816]{2,1,0:T(8,128)(2,1)S(1)} %collective-permute-done.5.got_ref), custom_call_target="tpu_custom_call" | custom-call | bytes 10000 | tf_op jit(solution)/shard_map/pallas_call | solution.py:354
  76.1 0.0 collective-permute-done.6.other_ref
  76.1 1.2 %shard_map.75 = (f32[864,64]{1,0:T(8,128)}, f32[1728,64]{1,0:T(8,128)}) custom-call(bf16[768,128]{1,0:T(8,128)(2,1)S(1)} %bitcast.11, bf16[768,128]{1,0:T(8,128)(2,1)S(1)} %collective-permute-done.6.other_ref), custom_call_target="tpu_custom_call" | custom-call | flops 2000000000 | bytes 4000000 | tf_op jit(solution)/shard_map/pallas_call | solution.py:347
  (4 shorter events, 0.1 us)
Async XLA Ops:
  0.6 16.0 %copy-start = (bf16[1,32,4,16,128]{4,3,2,1,0:T(8,128)(2,1)S(1)}, bf16[1,32,4,16,128]{4,3,2,1,0:T(8,128)(2,1)}, u32[]{:S(2)}) copy-start(bf16[1,32,4,16,128]{4,3,2,1,0:T(8,128)(2,1)} %v_ref.3) | copy-start | bytes 1572868
  0.6 16.0 %copy-start.1 = (bf16[27,64,64]{2,1,0:T(8,128)(2,1)S(1)}, bf16[27,64,64]{2,1,0:T(8,128)(2,1)}, u32[]{:S(2)}) copy-start(bf16[27,64,64]{2,1,0:T(8,128)(2,1)} %param.6) | copy-start | bytes 663556
  0.7 16.0 %copy-start.2 = (bf16[27,32,64]{2,1,0:T(8,128)(2,1)S(1)}, bf16[27,32,64]{2,1,0:T(8,128)(2,1)}, u32[]{:S(2)}) copy-start(bf16[27,32,64]{2,1,0:T(8,128)(2,1)} %param.5) | copy-start | bytes 331780
  2.8 15.2 %collective-permute-start = (bf16[1,32,1,16,128]{4,3,2,1,0:T(8,128)(2,1)}, bf16[1,32,1,16,128]{4,3,2,1,0:T(8,128)(2,1)S(1)}, u32[]{:S(2)}, u32[]{:S(2)}) collective-permute-start(bf16[1,32,1,16,128]{4,3,2,1,0:T(8,128)(2,1)} %get-tuple-element.29), channel_id=1, source_target_pairs={{0,1},{1,2},{2,3},{3,4},{4,5},{5,6},{6,7},{8,9},{9,10},{10,11},{11... | collective-permute-start | bytes 393224 | tf_op jit(solution)/shard_map/ppermute | solution.py:279
  12.4 15.4 %all-to-all-start = ((bf16[8,8,2048]{2,1,0:T(8,128)(2,1)}), bf16[8,8,2048]{2,1,0:T(8,128)(2,1)S(1)}, u32[]{:S(2)}, u32[]{:S(2)}) async-start(bf16[8,8,2048]{2,1,0:T(8,128)(2,1)} %get-tuple-element.37), calls=%async_computation | async-start | bytes 524288 | tf_op jit(solution)/shard_map/all_to_all | solution.py:283
  19.7 10.2 %collective-permute-start.1 = (bf16[16,2048]{1,0:T(8,128)(2,1)S(1)}, bf16[16,2048]{1,0:T(8,128)(2,1)S(1)}, u32[]{:S(2)}, u32[]{:S(2)}) collective-permute-start(bf16[16,2048]{1,0:T(8,128)(2,1)S(1)} %get-tuple-element.39), channel_id=1, source_target_pairs={{0,2},{2,4},{4,6},{6,0},{1,3},{3,5},{5,7},{7,1},{8,10},{10,12},{12... | collective-permute-start | bytes 196616 | tf_op jit(solution)/shard_map/ppermute | solution.py:319
  21.3 8.7 %collective-permute-start.2 = (bf16[16,2048]{1,0:T(8,128)(2,1)S(1)}, bf16[16,2048]{1,0:T(8,128)(2,1)S(1)}, u32[]{:S(2)}, u32[]{:S(2)}) collective-permute-start(bf16[16,2048]{1,0:T(8,128)(2,1)S(1)} %get-tuple-element.40), channel_id=1, source_target_pairs={{0,4},{2,6},{4,0},{6,2},{1,5},{3,7},{5,1},{7,3},{8,12},{10,14},{12... | collective-permute-start | bytes 196616 | tf_op jit(solution)/shard_map/ppermute | solution.py:319
  23.7 6.3 %collective-permute-start.3 = (bf16[16,2048]{1,0:T(8,128)(2,1)S(1)}, bf16[16,2048]{1,0:T(8,128)(2,1)S(1)}, u32[]{:S(2)}, u32[]{:S(2)}) collective-permute-start(bf16[16,2048]{1,0:T(8,128)(2,1)S(1)} %get-tuple-element.41), channel_id=1, source_target_pairs={{0,6},{2,0},{4,2},{6,4},{1,7},{3,1},{5,3},{7,5},{8,14},{10,8},{12,... | collective-permute-start | bytes 196616 | tf_op jit(solution)/shard_map/ppermute | solution.py:319
  29.9 3.1 %collective-permute-start.4 = (bf16[768,128]{1,0:T(8,128)(2,1)S(1)}, bf16[768,128]{1,0:T(8,128)(2,1)S(1)}, u32[]{:S(2)}, u32[]{:S(2)}) collective-permute-start(bf16[768,128]{1,0:T(8,128)(2,1)S(1)} %get-tuple-element.47), channel_id=1, source_target_pairs={{0,8},{8,0},{1,9},{9,1},{2,10},{10,2},{3,11},{11,3},{4,12},{12,4},... | collective-permute-start | bytes 589832 | tf_op jit(solution)/shard_map/ppermute | solution.py:334
  33.7 11.9 %all-to-all-start.1 = ((bf16[16,48,128]{2,1,0:T(8,128)(2,1)}), bf16[16,48,128]{2,1,0:T(8,128)(2,1)S(1)}, u32[]{:S(2)}, u32[]{:S(2)}) async-start(bf16[16,48,128]{2,1,0:T(8,128)(2,1)} %bitcast.3), calls=%async_computation.1 | async-start | bytes 393216 | tf_op jit(solution)/shard_map/all_to_all | solution.py:283
  38.6 21.7 %collective-permute-start.5 = (bf16[4,8,2816]{2,1,0:T(8,128)(2,1)S(1)}, bf16[4,8,2816]{2,1,0:T(8,128)(2,1)S(1)}, u32[]{:S(2)}, u32[]{:S(2)}) collective-permute-start(bf16[4,8,2816]{2,1,0:T(8,128)(2,1)S(1)} %get-tuple-element.50), channel_id=1, source_target_pairs={{0,1},{1,0},{2,3},{3,2},{4,5},{5,4},{6,7},{7,6},{8,9},{9,8},{10,11... | collective-permute-start | bytes 540680 | tf_op jit(solution)/shard_map/ppermute | solution.py:342
  71.8 4.4 %collective-permute-start.6 = (bf16[768,128]{1,0:T(8,128)(2,1)S(1)}, bf16[768,128]{1,0:T(8,128)(2,1)S(1)}, u32[]{:S(2)}, u32[]{:S(2)}) collective-permute-start(bf16[768,128]{1,0:T(8,128)(2,1)S(1)} %bitcast.10), channel_id=1, source_target_pairs={{0,8},{8,0},{1,9},{9,1},{2,10},{10,2},{3,11},{11,3},{4,12},{12,4},... | collective-permute-start | bytes 589832 | tf_op jit(solution)/shard_map/ppermute | solution.py:346

commit v6 on v5

--- a/solution.py
+++ b/solution.py
@@ -176,15 +176,15 @@
     row, col = cell_index(shape)
     spread = jnp.dot(two_ref[...], depths[...], preferred_element_type=F)
     total = None
-    for c in range(3):
-        side = None
-        for b in range(3):
+    for b in range(3):
+        line = None
+        for c in range(3):
             at = (3 * b + c) * C1
             part = spread[at : at + C1, :]
-            part = part if b == 1 else shifted(part, row, 1 - b, col, 0)
-            side = part if side is None else side + part
-        side = side if c == 1 else shifted(side, row, 0, col, 1 - c)
-        total = side if total is None else total + side
+            part = part if c == 1 else shifted(part, row, 0, col, 1 - c)
+            line = part if line is None else line + part
+        line = line if b == 1 else shifted(line, row, 1 - b, col, 0)
+        total = line if total is None else total + line
     grad_act = total.astype(BF).astype(F)
     act = act_ref[...].astype(F)
     grad_pre = (grad_act * jnp.where(act > 0, 1.0, SLOPE)).astype(BF)

time: 77.7 us -> 77.7 us (level)
  no operation moved by 1% of the time
where the time goes in v6:
time: 77.7 us; the launch traced here: 77.4 us
  starting transfers between devices  34.4 us (44%)
  blocking collectives  26.1 us (34%)
  Pallas kernels  9.68 us (12%)
  waiting for transfers between devices  5.62 us (7%)
    all_to_all x2, blocking collectives, exchange(): return lax.all_to_all(value, axes, split_axis=0, concat_axis=0, tiled=True)  26.1 us
    ppermute x1, starting transfers between devices, along(): return lax.ppermute(value, SPACE, pairs)  9.65 us
    all_to_all x2, starting transfers between devices, exchange(): return lax.all_to_all(value, axes, split_axis=0, concat_axis=0, tiled=True)  9.03 us
    ppermute x1, starting transfers between devices, shards(): got = lax.ppermute(send, 'zh', [(0, 1), (1, 0)])  5.46 us
    ppermute x3, starting transfers between devices, shards(): lax.ppermute(sent[step], 'y', [(at, (at + step) % 4) for at in range(4)])  5.11 us
    all_to_all x2, waiting for transfers between devices, exchange(): return lax.all_to_all(value, axes, split_axis=0, concat_axis=0, tiled=True)  4.59 us
    ppermute x1, starting transfers between devices, shards(): other_half = lax.ppermute(my_half, 'core', pairs)  3.21 us
    pallas_call x1, Pallas kernels, shards(): call(pack_inputs, [sds((8, 8, 2048), BF), sds((1, C0, 1, 16, 128), BF)],...  2.12 us
  transfers between devices with their start and end apart: 9, of which 3 were waited for; matrix products, arithmetic and copies ran while one was open for 0% of the time, Pallas kernels for 8%

profile of v6, /device:TPU:1, one launch (start us, length us, event | category | flops | bytes accessed | tf_op | source)
XLA Modules:
  0.0 77.4 jit_solution(12846660536997539193)
XLA Ops:
  0.6 0.0 copy-start
  0.6 0.0 copy-start.1
  0.7 0.0 copy-start.2
  0.7 2.1 %shard_map.67 = (bf16[8,8,2048]{2,1,0:T(8,128)(2,1)}, bf16[1,32,1,16,128]{4,3,2,1,0:T(8,128)(2,1)}) custom-call(bf16[1,8,16,8,64]{4,3,2,1,0:T(8,128)(2,1)} %x_ref.1, bf16[1,32,4,16,128]{4,3,2,1,0:T(8,128)(2,1)} %v_ref.3), custom_call_target="tpu_custom_call" | custom-call | bytes 4000000 | tf_op jit(solution)/shard_map/pallas_call | solution.py:291
  2.8 9.6 %collective-permute-start = (bf16[1,32,1,16,128]{4,3,2,1,0:T(8,128)(2,1)}, bf16[1,32,1,16,128]{4,3,2,1,0:T(8,128)(2,1)S(1)}, u32[]{:S(2)}, u32[]{:S(2)}) collective-permute-start(bf16[1,32,1,16,128]{4,3,2,1,0:T(8,128)(2,1)} %get-tuple-element.29), channel_id=1, source_target_pairs={{0,1},{1,2},{2,3},{3,4},{4,5},{5,6},{6,7},{8,9},{9,10},{10,11},{11... | collective-permute-start | bytes 393224 | tf_op jit(solution)/shard_map/ppermute | solution.py:279
  12.4 4.2 %all-to-all-start = ((bf16[8,8,2048]{2,1,0:T(8,128)(2,1)}), bf16[8,8,2048]{2,1,0:T(8,128)(2,1)S(1)}, u32[]{:S(2)}, u32[]{:S(2)}) async-start(bf16[8,8,2048]{2,1,0:T(8,128)(2,1)} %get-tuple-element.37), calls=%async_computation | async-start | bytes 524288 | tf_op jit(solution)/shard_map/all_to_all | solution.py:283
  16.6 0.0 copy-done
  16.7 1.3 %shard_map.68 = (bf16[288,512]{1,0:T(8,128)(2,1)S(1)}, bf16[576,1024]{1,0:T(8,128)(2,1)S(1)}, bf16[864,64]{1,0:T(8,128)(2,1)S(1)}, bf16[576,192]{1,0:T(8,128)(2,1)S(1)}) custom-call(bf16[1,32,4,16,128]{4,3,2,1,0:T(8,128)(2,1)S(1)} %copy-done, bf16[864,64]{1,0:T(8,128)(2,1)S(1)} %bitcast.9, bf16[1728,64]{1,0:T(8,128)(2,1)S(1)} %bitcast.8), custom_call_target="tpu_custom_call" | custom-call | bytes 12000000 | tf_op jit(solution)/shard_map/pallas_call | solution.py:303
  18.0 0.0 collective-permute-done.h_ref
  18.0 1.7 %shard_map.69 = (bf16[288,512]{1,0:T(8,128)(2,1)S(1)}, bf16[64,1024]{1,0:T(8,128)(2,1)S(1)}, f32[16,2048]{1,0:T(8,128)S(1)}, bf16[16,2048]{1,0:T(8,128)(2,1)S(1)...) custom-call(bf16[1,32,1,16,128]{4,3,2,1,0:T(8,128)(2,1)S(1)} %collective-permute-done.h_ref, ...), custom_call_target="tpu_custom_call" | custom-call | flops 10000000000 | bytes 8000000 | tf_op jit(solution)/shard_map/pallas_call | solution.py:311
  19.7 1.5 %collective-permute-start.1 = (bf16[16,2048]{1,0:T(8,128)(2,1)S(1)}, bf16[16,2048]{1,0:T(8,128)(2,1)S(1)}, u32[]{:S(2)}, u32[]{:S(2)}) collective-permute-start(bf16[16,2048]{1,0:T(8,128)(2,1)S(1)} %get-tuple-element.39), channel_id=1, source_target_pairs={{0,2},{2,4},{4,6},{6,0},{1,3},{3,5},{5,7},{7,1},{8,10},{10,12},{12... | collective-permute-start | bytes 196616 | tf_op jit(solution)/shard_map/ppermute | solution.py:319
  21.3 2.4 %collective-permute-start.2 = (bf16[16,2048]{1,0:T(8,128)(2,1)S(1)}, bf16[16,2048]{1,0:T(8,128)(2,1)S(1)}, u32[]{:S(2)}, u32[]{:S(2)}) collective-permute-start(bf16[16,2048]{1,0:T(8,128)(2,1)S(1)} %get-tuple-element.40), channel_id=1, source_target_pairs={{0,4},{2,6},{4,0},{6,2},{1,5},{3,7},{5,1},{7,3},{8,12},{10,14},{12... | collective-permute-start | bytes 196616 | tf_op jit(solution)/shard_map/ppermute | solution.py:319
  23.7 1.2 %collective-permute-start.3 = (bf16[16,2048]{1,0:T(8,128)(2,1)S(1)}, bf16[16,2048]{1,0:T(8,128)(2,1)S(1)}, u32[]{:S(2)}, u32[]{:S(2)}) collective-permute-start(bf16[16,2048]{1,0:T(8,128)(2,1)S(1)} %get-tuple-element.41), channel_id=1, source_target_pairs={{0,6},{2,0},{4,2},{6,4},{1,7},{3,1},{5,3},{7,5},{8,14},{10,8},{12,... | collective-permute-start | bytes 196616 | tf_op jit(solution)/shard_map/ppermute | solution.py:319
  24.8 3.0 %all-to-all-done = bf16[8,8,2048]{2,1,0:T(8,128)(2,1)S(1)} async-done(((bf16[8,8,2048]{2,1,0:T(8,128)(2,1)}), bf16[8,8,2048]{2,1,0:T(8,128)(2,1)S(1)}, u32[]{:S(2)}, u32[]{:S(2)}) %all-to-all-start) | async-done | bytes 262176 | tf_op jit(solution)/shard_map/all_to_all | solution.py:283
  27.8 2.1 %shard_map.70 = (f32[768,128]{1,0:T(8,128)S(1)}, bf16[768,128]{1,0:T(8,128)(2,1)S(1)}) custom-call(bf16[288,512]{1,0:T(8,128)(2,1)S(1)} %get-tuple-element.35.u_ref, bf16[288,512]{1,0:T(8,128)(2,1)S(1)} %get-tuple-element.30.zero_ref, bf16[576,1024]{1,0:T(8,128)(2,1)S(1)} %get-tuple-element.31.rest_ref, bf16[64,1024]{1,0:T(8,128)(2,1)S(1)} %get-tuple-element.36.act_ref, ...), custom_call_target="tpu_custom_call" | custom-call | bytes 12000000 | tf_op jit(solution)/shard_map/pallas_call | solution.py:321
  29.9 0.0 collective-permute-done.1.one_ref
  29.9 0.0 collective-permute-done.2.two_ref
  29.9 0.0 collective-permute-done.3.three_ref
  29.9 2.0 %collective-permute-start.4 = (bf16[768,128]{1,0:T(8,128)(2,1)S(1)}, bf16[768,128]{1,0:T(8,128)(2,1)S(1)}, u32[]{:S(2)}, u32[]{:S(2)}) collective-permute-start(bf16[768,128]{1,0:T(8,128)(2,1)S(1)} %get-tuple-element.47), channel_id=1, source_target_pairs={{0,8},{8,0},{1,9},{9,1},{2,10},{10,2},{3,11},{11,3},{4,12},{12,4},... | collective-permute-start | bytes 589832 | tf_op jit(solution)/shard_map/ppermute | solution.py:334
  31.9 0.1 shard_map.71
  32.0 1.0 %collective-permute-done.4 = bf16[768,128]{1,0:T(8,128)(2,1)S(1)} collective-permute-done((bf16[768,128]{1,0:T(8,128)(2,1)S(1)}, bf16[768,128]{1,0:T(8,128)(2,1)S(1)}, u32[]{:S(2)}, u32[]{:S(2)}) %collective-permute-start.4) | collective-permute-done | bytes 196640 | tf_op jit(solution)/shard_map/ppermute | solution.py:334
  33.0 0.7 add_convert_fusion
  33.7 4.8 %all-to-all-start.1 = ((bf16[16,48,128]{2,1,0:T(8,128)(2,1)}), bf16[16,48,128]{2,1,0:T(8,128)(2,1)S(1)}, u32[]{:S(2)}, u32[]{:S(2)}) async-start(bf16[16,48,128]{2,1,0:T(8,128)(2,1)} %bitcast.3), calls=%async_computation.1 | async-start | bytes 393216 | tf_op jit(solution)/shard_map/all_to_all | solution.py:283
  38.6 5.5 %collective-permute-start.5 = (bf16[4,8,2816]{2,1,0:T(8,128)(2,1)S(1)}, bf16[4,8,2816]{2,1,0:T(8,128)(2,1)S(1)}, u32[]{:S(2)}, u32[]{:S(2)}) collective-permute-start(bf16[4,8,2816]{2,1,0:T(8,128)(2,1)S(1)} %get-tuple-element.50), channel_id=1, source_target_pairs={{0,1},{1,0},{2,3},{3,2},{4,5},{5,4},{6,7},{7,6},{8,9},{9,8},{10,11... | collective-permute-start | bytes 540680 | tf_op jit(solution)/shard_map/ppermute | solution.py:342
  44.0 1.6 %all-to-all-done.1.x_ref = bf16[16,48,128]{2,1,0:T(8,128)(2,1)S(1)} async-done(((bf16[16,48,128]{2,1,0:T(8,128)(2,1)}), bf16[16,48,128]{2,1,0:T(8,128)(2,1)S(1)}, u32[]{:S(2)}, u32[]{:S(2)}) %all-to-all-start.1) | async-done | bytes 196640 | tf_op jit(solution)/shard_map/all_to_all | solution.py:283
  45.6 14.6 %all_to_all.20.x_ref = bf16[8,48,128]{2,1,0:T(8,128)(2,1)S(1)} all-to-all(bf16[8,48,128]{2,1,0:T(8,128)(2,1)S(1)} %shard_map.72), channel_id=1, replica_groups=mesh['zl'=4,'x'=4,'core'=2,'y'=4,'zh'=2] {'zl','zh'}, dimensions={0} | all-to-all | bytes 196608 | tf_op jit(solution)/shard_map/all_to_all | solution.py:283
  60.3 0.0 collective-permute-done.5.got_ref
  60.3 11.5 %all_to_all.21 = bf16[16,48,128]{2,1,0:T(8,128)(2,1)S(1)} all-to-all(bf16[16,48,128]{2,1,0:T(8,128)(2,1)S(1)} %shard_map.73), channel_id=1, replica_groups=mesh['zl'=4,'x'=4,'core'=2,'y'=4,'zh'=2] {'x','y'}, dimensions={0} | all-to-all | bytes 393216 | tf_op jit(solution)/shard_map/all_to_all | solution.py:283
  71.8 3.2 %collective-permute-start.6 = (bf16[768,128]{1,0:T(8,128)(2,1)S(1)}, bf16[768,128]{1,0:T(8,128)(2,1)S(1)}, u32[]{:S(2)}, u32[]{:S(2)}) collective-permute-start(bf16[768,128]{1,0:T(8,128)(2,1)S(1)} %bitcast.10), channel_id=1, source_target_pairs={{0,8},{8,0},{1,9},{9,1},{2,10},{10,2},{3,11},{11,3},{4,12},{12,4},... | collective-permute-start | bytes 589832 | tf_op jit(solution)/shard_map/ppermute | solution.py:346
  75.0 1.1 %shard_map.74 = bf16[1,8,16,8,64]{4,3,2,1,0:T(8,128)(2,1)} custom-call(f32[4,8,2048]{2,1,0:T(8,128)S(1)} %get-tuple-element.45.keep_ref, bf16[4,8,2816]{2,1,0:T(8,128)(2,1)S(1)} %collective-permute-done.5.got_ref), custom_call_target="tpu_custom_call" | custom-call | bytes 10000 | tf_op jit(solution)/shard_map/pallas_call | solution.py:354
  76.1 0.0 collective-permute-done.6.other_ref
  76.1 1.2 %shard_map.75 = (f32[864,64]{1,0:T(8,128)}, f32[1728,64]{1,0:T(8,128)}) custom-call(bf16[768,128]{1,0:T(8,128)(2,1)S(1)} %bitcast.11, bf16[768,128]{1,0:T(8,128)(2,1)S(1)} %collective-permute-done.6.other_ref), custom_call_target="tpu_custom_call" | custom-call | flops 2000000000 | bytes 4000000 | tf_op jit(solution)/shard_map/pallas_call | solution.py:347
  (4 shorter events, 0.1 us)
Async XLA Ops:
  0.6 16.0 %copy-start = (bf16[1,32,4,16,128]{4,3,2,1,0:T(8,128)(2,1)S(1)}, bf16[1,32,4,16,128]{4,3,2,1,0:T(8,128)(2,1)}, u32[]{:S(2)}) copy-start(bf16[1,32,4,16,128]{4,3,2,1,0:T(8,128)(2,1)} %v_ref.3) | copy-start | bytes 1572868
  0.6 16.0 %copy-start.1 = (bf16[27,64,64]{2,1,0:T(8,128)(2,1)S(1)}, bf16[27,64,64]{2,1,0:T(8,128)(2,1)}, u32[]{:S(2)}) copy-start(bf16[27,64,64]{2,1,0:T(8,128)(2,1)} %param.6) | copy-start | bytes 663556
  0.7 16.0 %copy-start.2 = (bf16[27,32,64]{2,1,0:T(8,128)(2,1)S(1)}, bf16[27,32,64]{2,1,0:T(8,128)(2,1)}, u32[]{:S(2)}) copy-start(bf16[27,32,64]{2,1,0:T(8,128)(2,1)} %param.5) | copy-start | bytes 331780
  2.8 15.2 %collective-permute-start = (bf16[1,32,1,16,128]{4,3,2,1,0:T(8,128)(2,1)}, bf16[1,32,1,16,128]{4,3,2,1,0:T(8,128)(2,1)S(1)}, u32[]{:S(2)}, u32[]{:S(2)}) collective-permute-start(bf16[1,32,1,16,128]{4,3,2,1,0:T(8,128)(2,1)} %get-tuple-element.29), channel_id=1, source_target_pairs={{0,1},{1,2},{2,3},{3,4},{4,5},{5,6},{6,7},{8,9},{9,10},{10,11},{11... | collective-permute-start | bytes 393224 | tf_op jit(solution)/shard_map/ppermute | solution.py:279
  12.4 15.4 %all-to-all-start = ((bf16[8,8,2048]{2,1,0:T(8,128)(2,1)}), bf16[8,8,2048]{2,1,0:T(8,128)(2,1)S(1)}, u32[]{:S(2)}, u32[]{:S(2)}) async-start(bf16[8,8,2048]{2,1,0:T(8,128)(2,1)} %get-tuple-element.37), calls=%async_computation | async-start | bytes 524288 | tf_op jit(solution)/shard_map/all_to_all | solution.py:283
  19.7 10.2 %collective-permute-start.1 = (bf16[16,2048]{1,0:T(8,128)(2,1)S(1)}, bf16[16,2048]{1,0:T(8,128)(2,1)S(1)}, u32[]{:S(2)}, u32[]{:S(2)}) collective-permute-start(bf16[16,2048]{1,0:T(8,128)(2,1)S(1)} %get-tuple-element.39), channel_id=1, source_target_pairs={{0,2},{2,4},{4,6},{6,0},{1,3},{3,5},{5,7},{7,1},{8,10},{10,12},{12... | collective-permute-start | bytes 196616 | tf_op jit(solution)/shard_map/ppermute | solution.py:319
  21.3 8.6 %collective-permute-start.2 = (bf16[16,2048]{1,0:T(8,128)(2,1)S(1)}, bf16[16,2048]{1,0:T(8,128)(2,1)S(1)}, u32[]{:S(2)}, u32[]{:S(2)}) collective-permute-start(bf16[16,2048]{1,0:T(8,128)(2,1)S(1)} %get-tuple-element.40), channel_id=1, source_target_pairs={{0,4},{2,6},{4,0},{6,2},{1,5},{3,7},{5,1},{7,3},{8,12},{10,14},{12... | collective-permute-start | bytes 196616 | tf_op jit(solution)/shard_map/ppermute | solution.py:319
  23.7 6.3 %collective-permute-start.3 = (bf16[16,2048]{1,0:T(8,128)(2,1)S(1)}, bf16[16,2048]{1,0:T(8,128)(2,1)S(1)}, u32[]{:S(2)}, u32[]{:S(2)}) collective-permute-start(bf16[16,2048]{1,0:T(8,128)(2,1)S(1)} %get-tuple-element.41), channel_id=1, source_target_pairs={{0,6},{2,0},{4,2},{6,4},{1,7},{3,1},{5,3},{7,5},{8,14},{10,8},{12,... | collective-permute-start | bytes 196616 | tf_op jit(solution)/shard_map/ppermute | solution.py:319
  29.9 3.1 %collective-permute-start.4 = (bf16[768,128]{1,0:T(8,128)(2,1)S(1)}, bf16[768,128]{1,0:T(8,128)(2,1)S(1)}, u32[]{:S(2)}, u32[]{:S(2)}) collective-permute-start(bf16[768,128]{1,0:T(8,128)(2,1)S(1)} %get-tuple-element.47), channel_id=1, source_target_pairs={{0,8},{8,0},{1,9},{9,1},{2,10},{10,2},{3,11},{11,3},{4,12},{12,4},... | collective-permute-start | bytes 589832 | tf_op jit(solution)/shard_map/ppermute | solution.py:334
  33.7 11.9 %all-to-all-start.1 = ((bf16[16,48,128]{2,1,0:T(8,128)(2,1)}), bf16[16,48,128]{2,1,0:T(8,128)(2,1)S(1)}, u32[]{:S(2)}, u32[]{:S(2)}) async-start(bf16[16,48,128]{2,1,0:T(8,128)(2,1)} %bitcast.3), calls=%async_computation.1 | async-start | bytes 393216 | tf_op jit(solution)/shard_map/all_to_all | solution.py:283
  38.6 21.7 %collective-permute-start.5 = (bf16[4,8,2816]{2,1,0:T(8,128)(2,1)S(1)}, bf16[4,8,2816]{2,1,0:T(8,128)(2,1)S(1)}, u32[]{:S(2)}, u32[]{:S(2)}) collective-permute-start(bf16[4,8,2816]{2,1,0:T(8,128)(2,1)S(1)} %get-tuple-element.50), channel_id=1, source_target_pairs={{0,1},{1,0},{2,3},{3,2},{4,5},{5,4},{6,7},{7,6},{8,9},{9,8},{10,11... | collective-permute-start | bytes 540680 | tf_op jit(solution)/shard_map/ppermute | solution.py:342
  71.8 4.4 %collective-permute-start.6 = (bf16[768,128]{1,0:T(8,128)(2,1)S(1)}, bf16[768,128]{1,0:T(8,128)(2,1)S(1)}, u32[]{:S(2)}, u32[]{:S(2)}) collective-permute-start(bf16[768,128]{1,0:T(8,128)(2,1)S(1)} %bitcast.10), channel_id=1, source_target_pairs={{0,8},{8,0},{1,9},{9,1},{2,10},{10,2},{3,11},{11,3},{4,12},{12,4},... | collective-permute-start | bytes 589832 | tf_op jit(solution)/shard_map/ppermute | solution.py:346
